TPU v7x, 32 devices: a whole 2x2x4 slice. The times are simulated.
32 devices in a mesh: seq: 16 (over z, y, x), head: 2 (over core).
Axes of the slice: x: 2, y: 2, z: 4, core: 2. Of those that a mesh axis runs over, the one named last changes fastest.
Arguments:
- hidden: float32 [2, 4096, 1536], P(None, 'seq'), may hold values from -6 to 6
- norm_gain: float32 [1536], replicated, may hold values from 0.5 to 1.5
- gate_weight: float32 [1536, 3072], P('seq', 'head'), may hold values from -0.15625 to 0.15625
- inner_weight: float32 [1536, 3072], P('seq', 'head'), may hold values from -0.15625 to 0.15625
- state_weight: float32 [1536, 256], P('seq'), may hold values from -0.15625 to 0.15625
- step_weight: float32 [1536, 48], P('seq', 'head'), may hold values from -0.15625 to 0.15625
- conv_weight: float32 [4, 3072], P(None, 'head'), may hold values from -3 to 3
- conv_bias: float32 [3072], P('head'), may hold values from -0.5 to 0.5
- state_conv_weight: float32 [4, 256], replicated, may hold values from -3 to 3
- state_conv_bias: float32 [256], replicated, may hold values from -0.5 to 0.5
- step_bias: float32 [48], P('head'), may hold values from -9.5 to -8.5
- log_rate: float32 [48], P('head'), may hold values from -3 to 5.5
- skip_gain: float32 [48], P('head'), may hold values from 0.5 to 1.5
- out_gain: float32 [3072], P('head'), may hold values from 0.5 to 1.5
- output_projection_weight: float32 [1536, 3072], P('seq', 'head'), may hold values from -0.109375 to 0.109375
- cotangent: float32 [2, 4096, 1536], P(None, 'seq'), may hold values from -6 to 6
Outputs:
- output: float32 [2, 4096, 1536], P(None, 'seq')
- hidden_grad: float32 [2, 4096, 1536], P(None, 'seq')
- norm_gain_grad: float32 [1536], replicated
- gate_weight_grad: float32 [1536, 3072], P('seq', 'head')
- inner_weight_grad: float32 [1536, 3072], P('seq', 'head')
- state_weight_grad: float32 [1536, 256], P('seq')
- step_weight_grad: float32 [1536, 48], P('seq', 'head')
- conv_weight_grad: float32 [4, 3072], P(None, 'head')
- conv_bias_grad: float32 [3072], P('head')
- state_conv_weight_grad: float32 [4, 256], replicated
- memory_filter_offset_derivative: float32 [256], replicated
- step_bias_grad: float32 [48], P('head')
- log_rate_grad: float32 [48], P('head')
- skip_gain_grad: float32 [48], P('head')
- out_gain_grad: float32 [3072], P('head')
- out_weight_grad: float32 [1536, 3072], P('seq', 'head')
All inputs are finite; a program needn't handle non-finite values.
Results may differ from a plain program's by a relative error of at most 0.005.
The roundings to bfloat16 on the way count: a program that leaves them out, or rounds other values in their place, can miss the bound.
Values may be sent and summed in bfloat16 or wider, within the bound.
No kernel may reach another device: no remote copies, remote signals or barrier semaphores. Data moves between devices by JAX's collectives and lax.ppermute only.
A program may use at most 256 MiB of HBM per device.

v0:
```python
import jax
import jax.numpy as jnp
from jax import lax
from jax.sharding import PartitionSpec as P

EPS = 1e-05


def from_behind(value, axis, by):
    size = lax.axis_size(axis)
    pairs = [(i, i + by) for i in range(size) if 0 <= i + by < size]
    return lax.ppermute(value, axis, pairs)


def entering(part, axis, combine, identity, reverse):
    count = lax.axis_size(axis)
    place = lax.axis_index(axis)
    ahead = count - 1 - place if reverse else place
    gathered = jax.tree.map(lambda a: lax.all_gather(a, axis), part)
    state = jax.tree.map(lambda a, e: jnp.zeros_like(a) + jnp.asarray(e, a.dtype), part, identity)

    def one(step, state):
        source = count - 1 - step if reverse else step
        return combine(
            state, jax.tree.map(lambda a: lax.dynamic_index_in_dim(a, source, 0, False), gathered)
        )

    return lax.fori_loop(0, ahead, one, state)


def fetch_inputs(gate_weight, inner_weight, state_weight, step_weight):
    return (
        lax.all_gather(gate_weight.astype(jnp.bfloat16), "seq", axis=0, tiled=True),
        lax.all_gather(inner_weight.astype(jnp.bfloat16), "seq", axis=0, tiled=True),
        lax.all_gather(state_weight.astype(jnp.bfloat16), "seq", axis=0, tiled=True),
        lax.all_gather(step_weight.astype(jnp.bfloat16), "seq", axis=0, tiled=True),
    )


def fetch_output(output_projection_weight):
    return lax.all_gather(output_projection_weight.astype(jnp.bfloat16), "seq", axis=0, tiled=True)


def carry_join(earlier, later):
    return (earlier[0] * later[0], later[1] + later[0][..., None, None] * earlier[1])


def silu_slope(values):
    sigma = jax.nn.sigmoid(values)
    return sigma * (1.0 + values * (1.0 - sigma))


def causal_decay(cumulative):
    length_q = cumulative.shape[1]
    row_index = lax.broadcasted_iota(jnp.int32, (length_q, length_q), 0)
    col_index = lax.broadcasted_iota(jnp.int32, (length_q, length_q), 1)
    return jnp.exp(
        jnp.where(row_index >= col_index, cumulative[:, :, None] - cumulative[:, None, :], -1e30)
    )


def intra_forward(pieces):
    inputs_x, write_in, read_in, step_size, cumulative = pieces
    low_x = inputs_x.astype(jnp.bfloat16)
    low_write = write_in.astype(jnp.bfloat16)
    low_read = read_in.astype(jnp.bfloat16)
    scores = jnp.einsum("tn,sn->ts", low_read, low_write, preferred_element_type=jnp.float32)
    decay_table = causal_decay(cumulative)
    weights = (scores[None] * decay_table * step_size[:, None, :]).astype(jnp.bfloat16)
    diagonal = jnp.einsum("hts,shp->thp", weights, low_x, preferred_element_type=jnp.float32)
    tail_weight = jnp.exp(cumulative[:, -1:] - cumulative) * step_size
    write_scaled = (write_in[None] * tail_weight[..., None]).astype(jnp.bfloat16)
    group_state = jnp.einsum(
        "hqn,qhp->hnp", write_scaled, low_x, preferred_element_type=jnp.float32
    )
    return (diagonal, group_state, jnp.exp(cumulative[:, -1]))


def intra_backward(pieces):
    inputs_x, write_in, read_in, step_size, cumulative, result_low, state_low = pieces
    low_x = inputs_x.astype(jnp.bfloat16)
    low_write = write_in.astype(jnp.bfloat16)
    low_read = read_in.astype(jnp.bfloat16)
    scores = jnp.einsum("tn,sn->ts", low_read, low_write, preferred_element_type=jnp.float32)
    decay_table = causal_decay(cumulative)
    exact_weights = scores[None] * decay_table * step_size[:, None, :]
    weights = exact_weights.astype(jnp.bfloat16)
    weights_grad = jnp.einsum("thp,shp->hts", result_low, low_x, preferred_element_type=jnp.float32)
    x_grad = jnp.einsum("hts,thp->shp", weights, result_low, preferred_element_type=jnp.float32)
    tail_decay = jnp.exp(cumulative[:, -1:] - cumulative)
    tail_weight = tail_decay * step_size
    write_scaled = (write_in[None] * tail_weight[..., None]).astype(jnp.bfloat16)
    scaled_grad = jnp.einsum("qhp,hnp->hqn", low_x, state_low, preferred_element_type=jnp.float32)
    x_grad = x_grad + jnp.einsum(
        "hqn,hnp->qhp", write_scaled, state_low, preferred_element_type=jnp.float32
    )
    score_low = jnp.sum(weights_grad * decay_table * step_size[:, None, :], axis=0).astype(
        jnp.bfloat16
    )
    read_grad = jnp.einsum("ts,sn->tn", score_low, low_write, preferred_element_type=jnp.float32)
    write_grad = jnp.einsum("ts,tn->sn", score_low, low_read, preferred_element_type=jnp.float32)
    write_grad = write_grad + jnp.sum(scaled_grad * tail_weight[..., None], axis=0)
    through = weights_grad * exact_weights
    cumulative_grad = jnp.sum(through, axis=2) - jnp.sum(through, axis=1)
    step_grad = jnp.sum(weights_grad * scores[None] * decay_table, axis=1)
    tail_grad = jnp.sum(scaled_grad * write_in[None], axis=2)
    step_grad = step_grad + tail_grad * tail_decay
    tail_through = tail_grad * tail_weight
    cumulative_grad = cumulative_grad - tail_through
    cumulative_grad = cumulative_grad.at[:, -1].add(jnp.sum(tail_through, axis=1))
    return (x_grad, write_grad, read_grad, cumulative_grad, step_grad)


def per_device(
    hidden,
    norm_gain,
    gate_weight,
    inner_weight,
    state_weight,
    step_weight,
    conv_weight,
    conv_bias,
    state_conv_weight,
    state_conv_bias,
    step_bias,
    log_rate,
    skip_gain,
    out_gain,
    output_projection_weight,
    cotangent,
):
    num_seqs, block_len, model_width = hidden.shape
    local_heads = step_bias.shape[0]
    inner_local = gate_weight.shape[1]
    head_width = inner_local // local_heads
    state_size = state_weight.shape[1] // 2
    kernel_size = conv_weight.shape[0]
    inner_total = inner_local * lax.axis_size("head")
    token_rows = num_seqs * block_len
    gate_rows, inner_rows, state_rows, step_rows = fetch_inputs(
        gate_weight, inner_weight, state_weight, step_weight
    )
    out_rows = fetch_output(output_projection_weight)
    inv_rms = lax.rsqrt(jnp.mean(hidden * hidden, axis=-1, keepdims=True) + EPS)
    unit_rows = hidden * inv_rms
    rescaled_activations = (unit_rows * norm_gain).astype(jnp.bfloat16)
    gate_pre = jnp.einsum(
        "sqd,dc->sqc", rescaled_activations, gate_rows, preferred_element_type=jnp.float32
    )
    inner_pre = jnp.einsum(
        "sqd,dc->sqc", rescaled_activations, inner_rows, preferred_element_type=jnp.float32
    )
    state_pre = jnp.einsum(
        "sqd,dc->sqc", rescaled_activations, state_rows, preferred_element_type=jnp.float32
    )
    step_raw = jnp.einsum(
        "sqd,dc->sqc", rescaled_activations, step_rows, preferred_element_type=jnp.float32
    )
    channels = jnp.concatenate([inner_pre, state_pre], axis=-1)
    boundary_lines = from_behind(channels[:, block_len - (kernel_size - 1) :], "seq", 1)
    padded = jnp.concatenate([boundary_lines, channels], axis=1)
    kernel = jnp.concatenate([conv_weight, state_conv_weight], axis=-1)
    conv_offset = jnp.concatenate([conv_bias, state_conv_bias], axis=-1)
    conv_out = conv_offset + sum(
        (
            kernel[tap_index] * padded[:, tap_index : tap_index + block_len]
            for tap_index in range(kernel_size)
        )
    )
    activated = jax.nn.silu(conv_out)
    inputs_x = activated[..., :inner_local].reshape(num_seqs, block_len, local_heads, head_width)
    write_in = activated[..., inner_local : inner_local + state_size]
    read_in = activated[..., inner_local + state_size :]
    pre_step = jnp.swapaxes(step_raw + step_bias, 1, 2)
    step_size = jax.nn.softplus(pre_step)
    decay_rate = -jnp.exp(log_rate)
    cumulative = jnp.cumsum(step_size * decay_rate[None, :, None], axis=2)
    diagonal, group_state, group_decay = lax.map(
        intra_forward, (inputs_x, write_in, read_in, step_size, cumulative)
    )
    identity = (jnp.ones_like(group_decay), jnp.zeros_like(group_state))
    incoming = entering((group_decay, group_state), "seq", carry_join, identity, False)[1]
    low_incoming = incoming.astype(jnp.bfloat16)
    growth = jnp.exp(cumulative)
    read_scaled = (read_in[:, None] * growth[..., None]).astype(jnp.bfloat16)
    offdiag = jnp.einsum(
        "shqn,shnp->sqhp", read_scaled, low_incoming, preferred_element_type=jnp.float32
    )
    mixer = diagonal + offdiag + skip_gain[:, None] * inputs_x
    mixer_flat = mixer.reshape(num_seqs, block_len, inner_local)
    gate_act = jax.nn.silu(gate_pre)
    gated = mixer_flat * gate_act
    square_sum = lax.psum(jnp.sum(gated * gated, axis=-1), "head")
    scaling_factor = lax.rsqrt(square_sum / inner_total + EPS)[..., None]
    scaled = gated * scaling_factor
    mixed_output = (scaled * out_gain).astype(jnp.bfloat16)
    out_terms = jnp.einsum(
        "sqc,dc->sqd", mixed_output, out_rows, preferred_element_type=jnp.float32
    )
    output = hidden + lax.psum(out_terms, "head")
    back_rows = fetch_inputs(gate_weight, inner_weight, state_weight, step_weight)
    back_out = fetch_output(output_projection_weight)
    back_gate, back_inner, back_state, back_step = back_rows
    cot_low = cotangent.astype(jnp.bfloat16)
    flat_mixed = mixed_output.reshape(token_rows, inner_local)
    flat_cot = cot_low.reshape(token_rows, model_width)
    columns = flat_cot
    out_weight_grad = lax.psum_scatter(
        jnp.einsum("rd,rc->dc", columns, flat_mixed, preferred_element_type=jnp.float32),
        "seq",
        scatter_dimension=0,
        tiled=True,
    )
    mixed_grad = jnp.einsum("sqd,dc->sqc", cot_low, back_out, preferred_element_type=jnp.float32)
    out_gain_local = jnp.sum(mixed_grad * scaled, axis=(0, 1))
    scaled_grad = mixed_grad * out_gain
    cross = lax.psum(jnp.sum(scaled_grad * gated, axis=-1), "head")
    gated_grad = (
        scaling_factor * scaled_grad
        - gated
        * (scaling_factor * scaling_factor * scaling_factor)
        * (cross / inner_total)[..., None]
    )
    blender_derivative = (gated_grad * gate_act).reshape(
        num_seqs, block_len, local_heads, head_width
    )
    valve_derivative = gated_grad * mixer_flat * silu_slope(gate_pre)
    mixer_low = blender_derivative.astype(jnp.bfloat16)
    skip_local = jnp.sum(blender_derivative * inputs_x, axis=(0, 1, 3))
    read_grad = jnp.einsum(
        "sqhp,shnp->shqn", mixer_low, low_incoming, preferred_element_type=jnp.float32
    )
    incoming_local = jnp.einsum(
        "shqn,sqhp->shnp", read_scaled, mixer_low, preferred_element_type=jnp.float32
    )
    outgoing_grad = entering((group_decay, incoming_local), "seq", carry_join, identity, True)[1]
    total_grad = jnp.sum(outgoing_grad * incoming, axis=(2, 3))
    state_low = outgoing_grad.astype(jnp.bfloat16)
    x_grad, write_grad, read_part, cumulative_grad, step_grad = lax.map(
        intra_backward, (inputs_x, write_in, read_in, step_size, cumulative, mixer_low, state_low)
    )
    x_grad = x_grad + skip_gain[:, None] * blender_derivative
    read_total = read_part + jnp.sum(read_grad * growth[..., None], axis=1)
    cumulative_grad = cumulative_grad + growth * jnp.sum(read_grad * read_in[:, None], axis=3)
    cumulative_grad = cumulative_grad.at[:, :, -1].add(total_grad * group_decay)
    rate_grad = lax.cumsum(cumulative_grad, axis=2, reverse=True)
    step_grad = step_grad + rate_grad * decay_rate[None, :, None]
    log_rate_local = jnp.sum(rate_grad * step_size, axis=(0, 2)) * decay_rate
    pre_grad = step_grad * jax.nn.sigmoid(pre_step)
    step_bias_local = jnp.sum(pre_grad, axis=(0, 2))
    raw_grad = jnp.swapaxes(pre_grad, 1, 2)
    write_sum, read_sum = lax.psum((write_grad, read_total), "head")
    act_grad = jnp.concatenate(
        [x_grad.reshape(num_seqs, block_len, inner_local), write_sum, read_sum], axis=-1
    )
    conv_grad = act_grad * silu_slope(conv_out)
    offset_grad = jnp.sum(conv_grad, axis=(0, 1))
    kernel_grad = jnp.stack(
        [
            jnp.sum(conv_grad * padded[:, tap_index : tap_index + block_len], axis=(0, 1))
            for tap_index in range(kernel_size)
        ]
    )
    padded_grad = jnp.zeros_like(padded)
    for tap_index in range(kernel_size):
        padded_grad = padded_grad.at[:, tap_index : tap_index + block_len].add(
            kernel[tap_index] * conv_grad
        )
    edge_grad = from_behind(padded_grad[:, : kernel_size - 1], "seq", -1)
    channel_grad = (
        padded_grad[:, kernel_size - 1 :].at[:, block_len - (kernel_size - 1) :].add(edge_grad)
    )
    proj_low = jnp.concatenate([valve_derivative, channel_grad, raw_grad], axis=-1).astype(
        jnp.bfloat16
    )
    gate_low = proj_low[..., :inner_local]
    inner_low = proj_low[..., inner_local : 2 * inner_local]
    state_pre_low = proj_low[..., 2 * inner_local : 2 * inner_local + 2 * state_size]
    step_low = proj_low[..., 2 * inner_local + 2 * state_size :]
    normed_local = jnp.einsum(
        "sqc,dc->sqd", gate_low, back_gate, preferred_element_type=jnp.float32
    )
    normed_local = normed_local + jnp.einsum(
        "sqc,dc->sqd", inner_low, back_inner, preferred_element_type=jnp.float32
    )
    normed_local = normed_local + jnp.einsum(
        "sqc,dc->sqd", step_low, back_step, preferred_element_type=jnp.float32
    )
    normed_grad = lax.psum(normed_local, "head")
    normed_grad = normed_grad + jnp.einsum(
        "sqc,dc->sqd", state_pre_low, back_state, preferred_element_type=jnp.float32
    )
    flat_normed = rescaled_activations.reshape(token_rows, model_width)
    flat_proj = proj_low.reshape(token_rows, proj_low.shape[-1])
    columns = flat_normed
    in_grad = lax.psum_scatter(
        jnp.einsum("rd,rc->dc", columns, flat_proj, preferred_element_type=jnp.float32),
        "seq",
        scatter_dimension=0,
        tiled=True,
    )
    gate_weight_grad = in_grad[:, :inner_local]
    inner_weight_grad = in_grad[:, inner_local : 2 * inner_local]
    state_weight_grad = in_grad[:, 2 * inner_local : 2 * inner_local + 2 * state_size]
    step_weight_grad = in_grad[:, 2 * inner_local + 2 * state_size :]
    norm_gain_local = jnp.sum(normed_grad * unit_rows, axis=(0, 1))
    unit_grad = normed_grad * norm_gain
    hidden_grad = (
        inv_rms * (unit_grad - unit_rows * jnp.mean(unit_grad * unit_rows, axis=-1, keepdims=True))
        + cotangent
    )
    summed = lax.psum(
        (
            norm_gain_local,
            kernel_grad[:, :inner_local],
            offset_grad[:inner_local],
            kernel_grad[:, inner_local:],
            offset_grad[inner_local:],
            step_bias_local,
            log_rate_local,
            skip_local,
            out_gain_local,
        ),
        "seq",
    )
    return (
        output,
        hidden_grad,
        summed[0],
        gate_weight_grad,
        inner_weight_grad,
        state_weight_grad,
        step_weight_grad,
        summed[1],
        summed[2],
        summed[3],
        summed[4],
        summed[5],
        summed[6],
        summed[7],
        summed[8],
        out_weight_grad,
    )


def solution(mesh):
    return jax.shard_map(
        per_device,
        mesh=mesh,
        in_specs=(
            P(None, "seq", None),
            P(),
            P("seq", "head"),
            P("seq", "head"),
            P("seq", None),
            P("seq", "head"),
            P(None, "head"),
            P("head"),
            P(),
            P(),
            P("head"),
            P("head"),
            P("head"),
            P("head"),
            P("seq", "head"),
            P(None, "seq", None),
        ),
        out_specs=(
            P(None, "seq", None),
            P(None, "seq", None),
            P(),
            P("seq", "head"),
            P("seq", "head"),
            P("seq", None),
            P("seq", "head"),
            P(None, "head"),
            P("head"),
            P(),
            P(),
            P("head"),
            P("head"),
            P("head"),
            P("head"),
            P("seq", "head"),
        ),
        check_vma=False,
    )
```

profile of v0, /device:TPU:0, one launch (start us, length us, event | category | flops | bytes accessed | tf_op | source)
XLA Modules:
  0.0 1717.9 jit_solution(5427200383202666025)
XLA Ops:
  10.9 43.4 %all-gather.3 = bf16[16,96,24]{1,2,0:T(8,128)(2,1)S(1)} all-gather(bf16[1,96,24]{1,2,0:T(8,128)(2,1)S(1)} %convert_bitcast_fusion.1), channel_id=1, replica_groups=mesh['seq'=16,'head'=2] {'seq'}, dimensions={0}, use_global_device_ids=true | all-gather | bytes 78336 | tf_op jit(solution)/shard_map/all_gather | solution.py:36
  62.4 45.4 %all_gather.41 = bf16[1536,256]{1,0:T(8,128)(2,1)S(1)} all-gather(bf16[96,256]{1,0:T(8,128)(2,1)S(1)} %convert_element_type.122), channel_id=1, replica_groups=mesh['seq'=16,'head'=2] {'seq'}, dimensions={0}, use_global_device_ids=true | all-gather | bytes 835584 | tf_op jit(solution)/shard_map/all_gather | solution.py:35
  136.1 18.3 %while.72 = (s32[]{:T(128)}, f32[2,256,24,64]{1,3,2,0:T(8,128)}, f32[2,24,128,64]{2,3,1,0:T(8,128)}, f32[2,24]{1,0:T(2,128)S(1)}, bf16[2,256,24,64]{1,3,2,0:T(8,...) while((s32[]{:T(128)}, f32[2,256,24,64]{1,3,2,0:T(8,128)}, ...), condition=%wide.region_4.5_spmd.clone, body=%wide.region_3.4_spmd.sunk.clone | while | flops 328282112 | bytes 18116320 | solution.py:178
  157.4 38.3 %all-gather.4 = f32[16,2,24]{2,1,0:T(2,128)S(1)} all-gather(f32[1,2,24]{2,1,0:T(2,128)S(1)} %bitcast.362), channel_id=3, replica_groups=mesh['seq'=16,'head'=2] {'seq'}, dimensions={0}, use_global_device_ids=true | all-gather | bytes 3264 | tf_op jit(solution)/shard_map/all_gather | solution.py:19
  195.7 230.1 %all-gather.17.cloned.1.call-done = f32[32,24,128,64]{2,3,1,0:T(8,128)} async-done(((f32[2,24,128,64]{2,3,1,0:T(8,128)}), f32[32,24,128,64]{2,3,1,0:T(8,128)}) %all-gather.17.cloned.1.call-update) | async-done | bytes 25165840 | tf_op jit(solution)/shard_map/all_gather | solution.py:19
  438.8 69.1 %all-gather.13.cloned.1.call-done = bf16[1536,1536]{1,0:T(8,128)(2,1)} async-done(((bf16[96,1536]{1,0:T(8,128)(2,1)}), bf16[1536,1536]{1,0:T(8,128)(2,1)}) %all-gather.13.cloned.1.call-update) | async-done | bytes 4718608 | tf_op jit(solution)/shard_map/all_gather | solution.py:33
  507.9 7.7 multiply_reduce_fusion.16
  518.0 72.2 %all-gather.15.cloned.1.call-done = bf16[1536,1536]{1,0:T(8,128)(2,1)} async-done(((bf16[96,1536]{1,0:T(8,128)(2,1)}), bf16[1536,1536]{1,0:T(8,128)(2,1)}) %all-gather.15.cloned.1.call-update) | async-done | bytes 4718608 | tf_op jit(solution)/shard_map/all_gather | solution.py:41
  590.2 9.4 multiply_reduce_fusion.10
  602.1 7.8 multiply_reduce_fusion.11
  624.1 8.1 fusion.79
  638.9 248.9 %all-gather.19.cloned.1.call-done = f32[32,24,128,64]{2,3,1,0:T(8,128)} async-done(((f32[2,24,128,64]{2,3,1,0:T(8,128)}), f32[32,24,128,64]{2,3,1,0:T(8,128)}) %all-gather.19.cloned.1.call-update) | async-done | bytes 25165840 | tf_op jit(solution)/shard_map/all_gather | solution.py:19
  889.8 131.9 %while.74 = (s32[]{:T(128)}, f32[2,24,128,64]{3,2,1,0:T(8,128)}, s32[]{:T(128)}, f32[16,2,24,128,64]{3,4,2,1,0:T(8,128)}, f32[16,2,24]{2,1,0:T(2,128)S(1)}) while((s32[]{:T(128)}, f32[2,24,128,64]{3,2,1,0:T(8,128)}, s32[]{:T(128)}, f32[16,2,24,128,64]{3,4,2,1,0:T(8,128)}, f32[16,2,24]{2,1,0:T(2,128)S(1)}) %tuple.252), condition=%wide.region_13.14_spmd.clone, body=%wide.region_12.13_spmd.sunk.clone | while | flops 786438 | bytes 11010739 | solution.py:28
  1030.4 61.7 %while.75 = (s32[]{:T(128)}, f32[2,256,24,64]{1,3,2,0:T(8,128)}, f32[2,256,128]{2,1,0:T(8,128)}, f32[2,256,128]{2,1,0:T(8,128)}, f32[2,24,256]{2,1,0:T(8,128)}, ...) while((s32[]{:T(128)}, f32[2,256,24,64]{1,3,2,0:T(8,128)}, ...), condition=%wide.region_23.24_spmd.clone, body=%wide.region_15.23_spmd.sunk.clone | while | flops 687810624 | bytes 52535400 | solution.py:239
  1116.0 9.0 fusion.124
  1131.4 10.1 scatter-add.22
  1147.0 10.1 scatter-add.25
  1179.2 14.1 convolution_bitcast_fusion.1
  1195.4 7.3 convolution_bitcast_fusion.2
  1202.6 10.3 copy.292
  1219.8 83.5 %all-reduce.1 = (f32[1536]{0:T(1024)}, f32[4,1536]{1,0:T(4,128)}, f32[1536]{0:T(1024)}, f32[4,256]{1,0:T(4,128)}, f32[256]{0:T(256)}, /*index=5*/f32[24]{0:T(128)}, f32[24]{0:T(128)}, f32[24]{0:T(128)}, f32[1536]{0:T(1024)}) all-reduce(f32[1536]{0:T(1024)S(1)} %get-tuple-element.793, ...), channel_id=1, replica_groups=mesh['seq'=16,'head'=2] {'seq'}, use_global_device_ids=true, to_apply=%region_34.35 | all-reduce | flops 12104 | bytes 96832 | tf_op jit(solution)/shard_map/psum | solution.py:312
  1303.4 7.5 multiply_add_fusion.1
  1310.9 222.9 %reduce-scatter.5.cloned.1.call-done = f32[96,3352]{1,0:T(8,128)} async-done(((f32[1536,3352]{1,0:T(8,128)}), f32[96,3352]{1,0:T(8,128)}) %reduce-scatter.5.cloned.1.call-update) | async-done | bytes 1287184 | tf_op jit(solution)/shard_map/reduce_scatter | solution.py:296
  1539.1 172.0 %reduce-scatter.7.cloned.1.call-done = f32[96,1536]{1,0:T(8,128)} async-done(((f32[1536,1536]{1,0:T(8,128)}), f32[96,1536]{1,0:T(8,128)}) %reduce-scatter.7.cloned.1.call-update) | async-done | bytes 589840
  (451 shorter events, 375.1 us)
Async XLA Ops:
  7.2 50.2 %copy-start.4 = (f32[2,256,1536]{2,1,0:T(8,128)S(1)}, f32[2,256,1536]{2,1,0:T(8,128)}, u32[]{:S(2)}) copy-start(f32[2,256,1536]{2,1,0:T(8,128)} %param.38) | copy-start | bytes 9437188
  7.2 50.2 %copy-start.59 = (f32[1536]{0:T(1024)S(1)}, f32[1536]{0:T(1024)}, u32[]{:S(2)}) copy-start(f32[1536]{0:T(1024)} %param.39) | copy-start | bytes 18436
  7.2 104.2 %all-gather.11.cloned.1.call-start = ((), (), s32[]{:S(2)}) async-start(), calls=%async_computation.2 | async-start | bytes 5013504 | tf_op jit(solution)/shard_map/all_gather | solution.py:34
  9.2 416.6 %all-gather.17.cloned.1.call-start = ((), (), s32[]{:S(2)}) async-start(), calls=%async_computation.6 | async-start | bytes 26738688 | tf_op jit(solution)/shard_map/all_gather | solution.py:19
  61.6 94.9 %copy-start.67 = (f32[2,24,2]{1,2,0:T(2,128)}, f32[2,24,2]{1,2,0:T(2,128)S(1)}, u32[]{:S(2)}) copy-start(f32[2,24,2]{1,2,0:T(2,128)S(1)} %slice.313) | copy-start | bytes 1156
  61.7 62.1 %copy-start.51 = (f32[1792]{0:T(1024)}, f32[1792]{0:T(1024)S(1)}, u32[]{:S(2)}) copy-start(f32[1792]{0:T(1024)S(1)} %get-tuple-element.805) | copy-start | bytes 21508
  61.7 62.1 %copy-start.53 = (f32[1792]{0:T(1024)}, f32[1792]{0:T(1024)S(1)}, u32[]{:S(2)}) copy-start(f32[1792]{0:T(1024)S(1)} %get-tuple-element.806) | copy-start | bytes 21508
  61.7 62.1 %copy-start.55 = (f32[1792]{0:T(1024)}, f32[1792]{0:T(1024)S(1)}, u32[]{:S(2)}) copy-start(f32[1792]{0:T(1024)S(1)} %get-tuple-element.807) | copy-start | bytes 21508
  61.7 62.1 %copy-start.57 = (f32[1792]{0:T(1024)}, f32[1792]{0:T(1024)S(1)}, u32[]{:S(2)}) copy-start(f32[1792]{0:T(1024)S(1)} %get-tuple-element.804) | copy-start | bytes 21508
  116.5 5.9 collective-permute-start
  154.5 353.4 %all-gather.13.cloned.1.call-start = ((), (), s32[]{:S(2)}) async-start(), calls=%async_computation.3 | async-start | bytes 5013504 | tf_op jit(solution)/shard_map/all_gather | solution.py:33
  155.3 434.9 %all-gather.15.cloned.1.call-start = ((), (), s32[]{:S(2)}) async-start(), calls=%async_computation.4 | async-start | bytes 5013504 | tf_op jit(solution)/shard_map/all_gather | solution.py:41
  156.4 731.5 %all-gather.19.cloned.1.call-start = ((), (), s32[]{:S(2)}) async-start(), calls=%async_computation.7 | async-start | bytes 26738688 | tf_op jit(solution)/shard_map/all_gather | solution.py:19
  435.0 72.8 %copy-start.13 = (bf16[2,256,1536]{2,1,0:T(8,128)(2,1)S(1)}, bf16[2,256,1536]{2,1,0:T(8,128)(2,1)}, u32[]{:S(2)}) copy-start(bf16[2,256,1536]{2,1,0:T(8,128)(2,1)} %copy-done.12) | copy-start | bytes 4718596
  438.8 151.4 %copy-start.70 = (f32[1536]{0:T(1024)S(1)}, f32[1536]{0:T(1024)}, u32[]{:S(2)}) copy-start(f32[1536]{0:T(1024)} %param.51) | copy-start | bytes 18436
  518.0 114.2 %copy-start.72 = (f32[2,256]{1,0:T(2,128)}, f32[2,256]{1,0:T(2,128)S(1)}, u32[]{:S(2)}) copy-start(f32[2,256]{1,0:T(2,128)S(1)} %get-tuple-element.921) | copy-start | bytes 6148
  617.8 498.1 %all-reduce.9.cloned.1.call-start = ((), (), s32[]{:S(2)}) async-start(), calls=%async_computation.10 | async-start | bytes 1048576 | tf_op jit(solution)/shard_map/psum | solution.py:252
  1030.4 61.7 %copy-start.68 = (f32[2,24,2]{1,2,0:T(2,128)S(1)}, f32[2,24,2]{1,2,0:T(2,128)}, u32[]{:S(2)}) copy-start(f32[2,24,2]{1,2,0:T(2,128)} %copy-done.67) | copy-start | bytes 1156
  1030.4 70.9 %copy-start.10 = (f32[2,256,1536]{1,2,0:T(8,128)S(1)}, f32[2,256,1536]{1,2,0:T(8,128)}, u32[]{:S(2)}) copy-start(f32[2,256,1536]{1,2,0:T(8,128)} %copy-done.9) | copy-start | bytes 9437188
  1101.2 112.9 %all-reduce.7.cloned.1.call-start = ((), (), s32[]{:S(2)}) async-start(), calls=%async_computation.9 | async-start | bytes 12582912 | tf_op jit(solution)/shard_map/psum | solution.py:200
  1109.9 65.5 %copy-start.47 = (bf16[2,24,256]{2,1,0:T(8,128)(2,1)}, bf16[2,24,256]{2,1,0:T(8,128)(2,1)S(1)}, u32[]{:S(2)}) copy-start(bf16[2,24,256]{2,1,0:T(8,128)(2,1)S(1)} %get-tuple-element.896) | copy-start | bytes 73732
  1158.0 6.1 collective-permute-start.1
  1177.8 356.0 %reduce-scatter.5.cloned.1.call-start = ((), (), s32[]{:S(2)}) async-start(), calls=%async_computation.5 | async-start | bytes 22560768 | tf_op jit(solution)/shard_map/reduce_scatter | solution.py:296
  1193.3 517.8 %reduce-scatter.7.cloned.1.call-start = ((), (), s32[]{:S(2)}) async-start(), calls=%async_computation.8 | async-start | bytes 10027008
  (86 other events, 377.4 us)
Sparse Core Ops, SparseCore 0:
  11.4 93.4 all-gather.10
  154.6 271.1 all-gather.16
  429.2 78.6 all-gather.12
  511.1 79.0 all-gather.14
  617.9 269.8 all-gather.18
  1101.3 14.6 all-reduce.8
  1177.9 34.4 all-reduce.6
  1218.3 315.4 reduce-scatter.4
  1541.0 170.0 reduce-scatter.6
where the time goes:
time: 1730 us; the launch traced here: 1720 us
  waiting for transfers between devices  1020 us (59%)
  blocking collectives  215 us (12%)
  local copies, waits for them, and re-layouts  180 us (10%)
  other arithmetic  143 us (8%)
  matrix products  134 us (8%)
    all_gather x2, waiting for transfers between devices, entering(): gathered = jax.tree.map(lambda a: lax.all_gather(a, axis), part)  479 us
    reduce_scatter x1, waiting for transfers between devices, per_device(): lax.psum_scatter(jnp.einsum('rd,rc->dc', columns, flat_proj, preferred_el...  223 us
    unnamed x10, waiting for transfers between devices  172 us
    psum x1, blocking collectives, per_device(): lax.psum((norm_gain_local, kernel_grad[:, :inner_local], offset_grad[:inn...  83.5 us
    dynamic_slice x30, local copies, waits for them, and re-layouts, one(): lax.dynamic_index_in_dim(a, source, 0, False)  73.2 us
    all_gather x1, waiting for transfers between devices, fetch_output(): lax.all_gather(output_projection_weight.astype(jnp.bfloat16), 'seq', axis...  72.2 us
    all_gather x1, waiting for transfers between devices, fetch_inputs(): lax.all_gather(gate_weight.astype(jnp.bfloat16), 'seq', axis=0, tiled=True)  69.1 us
    add x15, other arithmetic, carry_join(): later[1] + later[0][..., None, None] * earlier[1]  58.3 us
  transfers between devices with their start and end apart: 11, of which 9 were waited for; matrix products, arithmetic and copies ran while one was open for 7% of the time, Pallas kernels for 0%

commit v1 on v0

v1 whole, which is shorter than its diff:
```python
import functools
import math

import jax
import jax.numpy as jnp
from jax import lax
from jax.experimental import pallas as pl
from jax.experimental.pallas import tpu as pltpu
from jax.sharding import Mesh, PartitionSpec as P

EPS = 1e-05
WAYS = 4
LANES = 128
EDGE = 16
TILE = 128
MIB = 1024 * 1024
PLANE, PART, HEAD = "plane", "part", "head"
BLOCK, PLACE, SEQ, ALL = range(4)
F32 = jnp.float32
BF16 = jnp.bfloat16


def cost_of(us):
    return pl.CostEstimate(flops=1024, bytes_accessed=int(us * 3.5e6), transcendentals=0)


def mm(spec, a, b):
    return jnp.einsum(spec, a, b, preferred_element_type=F32)


def flip(value, axis, by):
    size = lax.axis_size(axis)
    return lax.ppermute(value, axis, [(i, i ^ by) for i in range(size)])


def shift(value, axis, by):
    size = lax.axis_size(axis)
    pairs = [(i, i + by) for i in range(size) if 0 <= i + by < size]
    return lax.ppermute(value, axis, pairs)


def total(value, axes, start=1):
    for axis in axes:
        step, start = start, 1
        while step < lax.axis_size(axis):
            value = value + flip(value, axis, step)
            step *= 2
    return value


def take(value, index, axis=0):
    return lax.dynamic_index_in_dim(value, index, axis, False)


def reorder(value, index):
    return jnp.stack([take(value, index[i]) for i in range(value.shape[0])])


def both_cores(value, core):
    other = flip(value, HEAD, 1)
    return jnp.where(core == 0, jnp.stack([value, other]), jnp.stack([other, value]))


def dot(a, b):
    return lax.dot_general(a, b, (((1,), (0,)), ((), ())), preferred_element_type=F32)


def dot_nt(a, b):
    return lax.dot_general(a, b, (((1,), (1,)), ((), ())), preferred_element_type=F32)


def dot_tn(a, b):
    return lax.dot_general(a, b, (((0,), (0,)), ((), ())), preferred_element_type=F32)


def terms_of(value, count):
    parts = []
    for _ in range(count):
        part = value.astype(BF16)
        parts.append(part)
        value = value - part.astype(F32)
    return parts


def fine_dot(product, a, b):
    left = terms_of(a, 2) if a.dtype == F32 else [a]
    right = terms_of(b, 2) if b.dtype == F32 else [b]
    value = product(left[0], right[0])
    for part in left[1:]:
        value = value + product(part, right[0])
    for part in right[1:]:
        value = value + product(left[0], part)
    return value


def triangle_sum(size, reverse, value):
    row = lax.broadcasted_iota(jnp.int32, (size, size), 0)
    col = lax.broadcasted_iota(jnp.int32, (size, size), 1)
    ones = jnp.where(row <= col if reverse else row >= col, 1.0, 0.0).astype(BF16)
    return sum(dot(ones, part) for part in terms_of(value, 3))


def head_lanes(cols, width):
    at = lax.broadcasted_iota(jnp.int32, (LANES, cols), 1) - width * lax.broadcasted_iota(
        jnp.int32, (LANES, cols), 0
    )
    return jnp.where(jnp.logical_and(at >= 0, at < width), 1.0, 0.0).astype(BF16)


def spread_heads(value, table):
    return sum(dot(part, table) for part in terms_of(value, 2))


def sum_heads(value, table):
    return sum(dot_nt(part, table) for part in terms_of(value, 2))


def pack(leaving, run, run_decay):
    cols = run.shape[0]
    leaving[0, :cols] = run[...]
    leaving[0, cols:] = run_decay[...]


def unpack(came, run, width):
    cols = run.shape[0]
    run[...] = jnp.zeros_like(run)
    for ref in reversed(came):
        decay = ref[0, cols : cols + 1]
        for h in range(cols // width):
            at = slice(h * width, (h + 1) * width)
            run[at] = ref[0, at] + decay[:, h : h + 1] * run[at]


def conv_kernel(width, order, pre, halo, taps, offset, step, rate, act, conv, cum, cum_t, step_t, state, leaving, ext, run, run_decay):
    b = pl.program_id(1)
    size, wide = conv.shape[1:]
    tail_rows = ext.shape[0] - size
    count = taps.shape[0]

    @pl.when(b == 0)
    def _():
        ext[:tail_rows] = halo[0]
        run[...] = jnp.zeros_like(run)
        run_decay[...] = jnp.ones_like(run_decay)

    @pl.when(b > 0)
    def _():
        ext[:tail_rows] = ext[size:]

    ext[tail_rows:] = pre[0, :, :wide]
    first = tail_rows - count + 1
    value = offset[...] + sum(taps[k : k + 1] * ext[first + k : first + k + size] for k in range(count))
    conv[0] = value
    active = value * jax.nn.sigmoid(value)
    act[0] = active
    cols = run.shape[0]
    lanes = run.shape[1]
    steps = step[0]
    total_decay = triangle_sum(size, False, steps * rate[...])
    cum[0] = total_decay
    cum_t[0] = total_decay.T[: cum_t.shape[1]]
    step_t[0] = steps.T[: cum_t.shape[1]]
    last = total_decay[size - 1 : size]
    tail = spread_heads(jnp.exp(last - total_decay) * steps, head_lanes(cols, width))
    decay = jnp.exp(last)
    scaled = (active[:, :cols].astype(BF16).astype(F32) * tail).T
    added = fine_dot(dot, scaled, active[:, cols : cols + lanes])
    state[0] = added
    for h in range(cols // width):
        at = slice(h * width, (h + 1) * width)
        run[at] = decay[:, h : h + 1] * run[at] + added[at]
    run_decay[...] = run_decay[...] * decay
    pack(leaving, run, run_decay)


def decay_block(column, row, masked):
    value = column - row
    if masked:
        at = lax.broadcasted_iota(jnp.int32, value.shape, 0)
        value = jnp.where(at >= lax.broadcasted_iota(jnp.int32, value.shape, 1), value, -1e30)
    return jnp.exp(value)


def diagonal_kernel(width, order, act, cum, cum_t, step_t, diagonal, scores, weights):
    size, cols = diagonal.shape[1:]
    lanes = (act.shape[2] - cols) // 2
    heads = cols // width
    low_x = act[0, :, :cols].astype(BF16)
    low_write = act[0, :, cols : cols + lanes].astype(BF16)
    low_read = act[0, :, cols + lanes :].astype(BF16)
    scores[...] = dot_nt(low_read, low_write)

    @pl.when(jnp.logical_and(pl.program_id(0) == 0, pl.program_id(1) == 0))
    def _():
        weights[...] = jnp.zeros_like(weights)

    for h in range(heads):
        for top in range(0, size, TILE):
            rows = slice(top, top + TILE)
            column = cum[0, rows, h : h + 1]
            for left in range(0, top + TILE, TILE):
                span = slice(left, left + TILE)
                table = decay_block(column, cum_t[0, h : h + 1, span], left == top)
                value = scores[rows, span] * table * step_t[0, h : h + 1, span]
                weights[h, rows, span] = value.astype(BF16)
        at = slice(h * width, (h + 1) * width)
        diagonal[0, :, at] = dot(weights[h], low_x[:, at])


def mixer_kernel(width, order, act, cum, diagonal, state, gate, grad, skip, gain, *rest):
    *came, mixer, incoming, sums, run = rest
    size, cols = mixer.shape[1:]
    lanes = run.shape[1]

    @pl.when(pl.program_id(1) == 0)
    def _():
        unpack(came, run, width)

    held = run[...]
    incoming[0] = held
    low_held = held.astype(BF16)
    growth = jnp.exp(cum[0])
    offdiag = fine_dot(dot_nt, act[0, :, cols + lanes :], low_held)
    offdiag = spread_heads(growth, head_lanes(cols, width)) * offdiag
    for h in range(cols // width):
        at = slice(h * width, (h + 1) * width)
        run[at] = growth[size - 1 : size, h : h + 1] * held[at] + state[0, at]
    mixed = diagonal[0] + offdiag + skip[...] * act[0, :, :cols]
    mixer[0] = mixed
    gates = gate[0]
    gated = mixed * (gates * jax.nn.sigmoid(gates))
    square = jnp.sum(gated * gated, axis=1, keepdims=True)
    cross = jnp.sum(grad[0] * gain[...] * gated, axis=1, keepdims=True)
    lane = lax.broadcasted_iota(jnp.int32, (size, LANES), 1)
    both = jnp.where(lane == 0, square, jnp.where(lane == 1, cross, 0.0))
    sums[0] = both.T[: sums.shape[1]]


def gate_kernel(width, inner_total, order, mixer, gate, grad, act, cum, sums, gain, mixed, mixer_grad, gate_low, add, leaving, gain_sum, skip_sum, run, run_decay):
    size, cols = mixed.shape[1:]
    lanes = run.shape[1]
    first = jnp.logical_and(pl.program_id(0) == 0, pl.program_id(1) == 0)

    @pl.when(first)
    def _():
        gain_sum[...] = jnp.zeros_like(gain_sum)
        skip_sum[...] = jnp.zeros_like(skip_sum)

    @pl.when(pl.program_id(1) == 0)
    def _():
        run[...] = jnp.zeros_like(run)
        run_decay[...] = jnp.ones_like(run_decay)

    turned = sums[0].T
    factor = lax.rsqrt(turned[:, 0:1] / inner_total + EPS)
    cross = turned[:, 1:2] / inner_total
    gates = gate[0]
    sigma = jax.nn.sigmoid(gates)
    opened = gates * sigma
    value = mixer[0]
    gated = value * opened
    scaled = gated * factor
    mixed[0] = (scaled * gain[...]).astype(BF16)
    grads = grad[0]
    gain_sum[...] += jnp.sum(grads * scaled, axis=0, keepdims=True)
    gated_grad = factor * (grads * gain[...]) - gated * (factor * factor * factor) * cross
    through = gated_grad * opened
    mixer_grad[0] = through
    gate_low[0] = (gated_grad * value * (sigma * (1.0 + gates * (1.0 - sigma)))).astype(BF16)
    skip_sum[...] += jnp.sum(through * act[0, :, :cols], axis=0, keepdims=True)
    growth = jnp.exp(cum[0])
    low = through.astype(BF16).astype(F32)
    grown = (low * spread_heads(growth, head_lanes(cols, width))).T
    added = fine_dot(dot, grown, act[0, :, cols + lanes :])
    add[0] = added
    for h in range(cols // width):
        at = slice(h * width, (h + 1) * width)
        run[at] = growth[size - 1 : size, h : h + 1] * run[at] + added[at]
    run_decay[...] = run_decay[...] * growth[size - 1 : size]
    pack(leaving, run, run_decay)


def back_kernel(
    width, order, act, conv, pre, cum, cum_t, step, step_t, sigma, mixer_grad, incoming, add, halo, taps, rate, skip, *rest
):
    *came, chan_low, edge, first_rows, taps_sum, bias_sum, rate_sum, step_sum, run, ext, scores, weights, score_sum, by_col = rest
    s, b = pl.program_id(0), pl.program_id(1)
    size, wide = act.shape[1:]
    cols, lanes = run.shape
    tail_rows = ext.shape[0] - size
    count = taps.shape[0]

    @pl.when(jnp.logical_and(s == 0, b == 0))
    def _():
        for ref in (taps_sum, bias_sum, rate_sum, step_sum):
            ref[...] = jnp.zeros_like(ref)

    @pl.when(b == 0)
    def _():
        unpack(came, run, width)
        ext[size:] = jnp.zeros((tail_rows, wide), F32)

    @pl.when(b > 0)
    def _():
        ext[size:] = ext[:tail_rows]

    heads = cols // width
    active = act[0]
    low_x = active[:, :cols].astype(BF16)
    low_write = active[:, cols : cols + lanes].astype(BF16)
    low_read = active[:, cols + lanes :].astype(BF16)
    scores[...] = dot_nt(low_read, low_write)
    outgoing = run[...]
    low_out = outgoing.astype(BF16)
    low_held = incoming[0].astype(BF16)
    grads = mixer_grad[0]
    low_grad = grads.astype(BF16)
    turned = grads.T.astype(BF16)
    decays = cum[0]
    last = decays[size - 1 : size]
    steps = step[0]
    growth = jnp.exp(decays)
    tail_decay = jnp.exp(last - decays)
    tail = tail_decay * steps
    block_decay = jnp.exp(last)

    @pl.when(jnp.logical_and(s == 0, b == 0))
    def _():
        weights[...] = jnp.zeros_like(weights)
        score_sum[...] = jnp.zeros_like(score_sum)
        by_col[...] = jnp.zeros_like(by_col)

    lane = lax.broadcasted_iota(jnp.int32, (TILE, LANES), 1)
    row_tiles = [jnp.zeros((TILE, LANES), F32) for _ in range(size // TILE)]
    pieces = []
    for h in range(heads):
        at = slice(h * width, (h + 1) * width)
        col = slice(h, h + 1)
        grads_w = dot_nt(low_grad[:, at], low_x[:, at])
        col_sums = [jnp.zeros((1, TILE), F32) for _ in range(size // TILE)]
        for i, top in enumerate(range(0, size, TILE)):
            rows = slice(top, top + TILE)
            column = decays[rows, col]
            across = jnp.zeros((TILE, TILE), F32)
            for j, left in enumerate(range(0, top + TILE, TILE)):
                span = slice(left, left + TILE)
                table = decay_block(column, cum_t[0, col, span], left == top)
                step_row = step_t[0, col, span]
                score = scores[rows, span]
                weights[h, rows, span] = (score * table * step_row).astype(BF16)
                eased = grads_w[rows, span] * table
                stepped = eased * step_row
                if h == 0:
                    score_sum[rows, span] = stepped
                else:
                    score_sum[rows, span] += stepped
                col_sums[j] = col_sums[j] + jnp.sum(eased * score, axis=0, keepdims=True)
                across = across + stepped * score
            row_tiles[i] = jnp.where(
                lane == h, jnp.sum(across, axis=1, keepdims=True), row_tiles[i]
            )
        by_col[col] = jnp.concatenate(col_sums, axis=1)
        pieces.append(dot(turned[at], weights[h]))
    by_row = jnp.concatenate(row_tiles, axis=0)

    table = head_lanes(cols, width)
    tail_all = spread_heads(tail, table)
    growth_all = spread_heads(growth, table)
    write_out = fine_dot(dot_nt, active[:, cols : cols + lanes], low_out)
    read_held = fine_dot(dot_nt, active[:, cols + lanes :], low_held)
    tail_grad = sum_heads(low_x.astype(F32) * write_out, table)
    read_dot = sum_heads(low_grad.astype(F32) * read_held, table)
    score_low = score_sum[...].astype(BF16)
    write_sum = fine_dot(dot, low_x.astype(F32) * tail_all, low_out)
    write_sum = write_sum + dot_tn(score_low, low_read)
    read_sum = fine_dot(dot, low_grad.astype(F32) * growth_all, low_held)
    read_sum = read_sum + dot(score_low, low_write)
    pair = jnp.sum(outgoing * incoming[0], axis=1, keepdims=True)
    lane_row = lax.broadcasted_iota(jnp.int32, (1, LANES), 1)
    state_dot = jnp.zeros((1, LANES), F32)
    for h in range(heads):
        at = slice(h * width, (h + 1) * width)
        col = slice(h, h + 1)
        state_dot = jnp.where(lane_row == h, jnp.sum(pair[at], axis=0, keepdims=True), state_dot)
        run[at] = block_decay[:, col] * outgoing[at] + add[0, at]

    pad = jnp.zeros((LANES - by_col.shape[0], size), F32)
    step_grad = jnp.concatenate([by_col[...], pad], axis=0).T
    tail_through = tail_grad * tail
    row_index = lax.broadcasted_iota(jnp.int32, (size, LANES), 0)
    at_last = jnp.sum(tail_through, axis=0, keepdims=True) + state_dot * block_decay
    cum_grad = by_row - steps * step_grad - tail_through + growth * read_dot
    cum_grad = cum_grad + jnp.where(row_index == size - 1, at_last, 0.0)
    rate_grad = triangle_sum(size, True, cum_grad)
    step_grad = step_grad + tail_grad * tail_decay + rate_grad * rate[...]
    rate_sum[...] += jnp.sum(rate_grad * steps, axis=0, keepdims=True) * rate[...]
    raw = step_grad * sigma[0]
    chan_low[0, :, wide:] = raw.astype(BF16)
    step_sum[...] += jnp.sum(raw, axis=0, keepdims=True)

    x_grad = jnp.concatenate(pieces, axis=0).T + write_out * tail_all + skip[...] * grads
    value = conv[0]
    sig = jax.nn.sigmoid(value)
    slope = sig * (1.0 + value * (1.0 - sig))
    conv_grad = jnp.concatenate([x_grad, write_sum, read_sum], axis=1) * slope
    ext[:size] = conv_grad
    bias_sum[...] += jnp.sum(conv_grad, axis=0, keepdims=True)
    channels = pre[0]
    channel_grad = jnp.zeros((size, wide), F32)
    for k in range(count):
        moved = ext[count - 1 - k : count - 1 - k + size]
        channel_grad = channel_grad + taps[k : k + 1] * moved
        taps_sum[k : k + 1] += jnp.sum(channels * moved, axis=0, keepdims=True)
    chan_low[0, :, :wide] = channel_grad.astype(BF16)

    @pl.when(b == 0)
    def _():
        edge[0] = channel_grad[size - EDGE :]

    @pl.when(b == pl.num_programs(1) - 1)
    def _():
        first_rows[0] = conv_grad[:8]
        for k in range(count - 1):
            have = count - 1 - k
            taps_sum[k : k + 1] += jnp.sum(
                halo[0, 8 - have :] * conv_grad[:have], axis=0, keepdims=True
            )


def gather_kernel(ranges, core, own, *refs):
    others = 2 * (WAYS - 1)
    near, far = refs[: WAYS - 1], refs[WAYS - 1 : others]
    table, tokens, *results = refs[others:]
    step = tokens.shape[0]
    sources = [None, *near, None, *far]
    for at in range(0, 2 * WAYS, step):

        @pl.when(pl.program_id(0) == at // step)
        def _(at=at):
            for j in range(step):
                ref = sources[at + j]
                if ref is None:
                    tokens[j] = own[lax.rem(core[0] + (at + j) // WAYS, 2)]
                else:
                    tokens[j] = ref[...]

    rows = flat_rows(tokens)
    for (at, size), result in zip(ranges, results):
        result[...] = dot(rows, table[:, at : at + size]).reshape(result.shape)


def rows_kernel(columns, tokens, table, result):
    at, size = columns
    result[...] = dot(flat_rows(tokens), table[:, at : at + size]).reshape(result.shape)


def join_kernel(ranges, summed, *refs):
    count = len(ranges)
    lows, arrived, tables, others = [refs[j * count : (j + 1) * count] for j in range(4)]
    value = None
    for low, table, at_size in zip((*lows, *arrived), (*tables, *others), ranges + ranges):
        at, size = at_size
        term = dot_nt(flat_rows(low), table[:, at : at + size])
        value = term if value is None else value + term
    if summed:
        tokens, keep_a, keep_b, send_a, send_b, gain_sum = refs[4 * count :]

        @pl.when(pl.program_id(0) == 0)
        def _():
            gain_sum[...] = jnp.zeros_like(gain_sum)

        gain_sum[...] += jnp.sum(value * flat_rows(tokens).astype(F32), axis=0, keepdims=True)
    else:
        keep_a, keep_b, send_a, send_b = refs[4 * count :]
    size, half = keep_a.shape[1:]

    @pl.when(pl.program_id(0) == 0)
    def _():
        keep_a[0] = value[:size, :half]
        keep_b[0] = value[:size, half:]
        send_a[0] = value[size:, :half].astype(BF16)
        keep_b[1] = value[size:, half:]

    @pl.when(pl.program_id(0) == 1)
    def _():
        keep_a[1] = value[:size, :half]
        send_b[0] = value[:size, half:].astype(BF16)
        send_a[1] = value[size:, :half].astype(BF16)
        send_b[1] = value[size:, half:].astype(BF16)


def middle_kernel(keep_a, keep_b, got_a, got_b, send_a, send_b):
    send_a[...] = (keep_a[0] + got_a[0].astype(F32)).astype(BF16)
    send_b[...] = (keep_b[0] + got_b[0].astype(F32)).astype(BF16)


def flat_rows(ref):
    value = ref[...]
    return value.reshape(value.shape[0] * value.shape[1], value.shape[2])


def store_tiles(result, at, value):
    count, _, deep = result.shape
    for i in range(count):
        result[i, at : at + value.shape[0]] = value[:, i * deep : (i + 1) * deep].astype(
            result.dtype
        )


def early_grad_kernel(tokens, gate_low, cot_low, mixed, result, turned):
    cols = gate_low.shape[2]

    @pl.when(pl.program_id(0) == 0)
    def _():
        turned[:cols] = flat_rows(gate_low).T
        turned[cols:] = flat_rows(mixed).T

    store_tiles(result, 0, dot(turned[:cols], flat_rows(tokens)))
    store_tiles(result, cols, dot(turned[cols:], flat_rows(cot_low)))


def late_grad_kernel(core, tokens, chan_low, inner, mine, other, step, turned):
    cols, lanes = inner.shape[1], mine.shape[1]
    wide = cols + 2 * lanes

    @pl.when(pl.program_id(0) == 0)
    def _():
        turned[...] = flat_rows(chan_low).T

    rows = flat_rows(tokens)
    store_tiles(inner, 0, dot(turned[:cols], rows))
    write = dot(turned[cols : cols + lanes], rows)
    read = dot(turned[cols + lanes : wide], rows)
    swap = core[0] != 0
    store_tiles(mine, 0, jnp.where(swap, read, write))
    store_tiles(other, 0, jnp.where(swap, write, read))
    store_tiles(step, 0, dot(turned[wide : wide + step.shape[1]], rows))


def chunk_kernel(plane, inner, mine, arrived, step, own, *sent):
    k = pl.program_id(0)
    cols, lanes = inner.shape[1], mine.shape[1]
    state = mine[0] + arrived[0]

    @pl.when(k == 0)
    def _():
        own[:cols] = inner[0].astype(F32)
        own[cols : cols + lanes] = state
        own[cols + lanes :] = step[0].astype(F32)

    for j, ref in enumerate(sent):

        @pl.when(k == j + 1)
        def _(ref=ref):
            ref[:cols] = inner[0]
            ref[cols : cols + lanes] = state.astype(BF16)
            ref[cols + lanes :] = step[0]


def turn_kernel(cols, lanes, part, early, own, *refs):
    count = (len(refs) - 1 - WAYS) if len(refs) > WAYS else 0
    value = own[...]
    for ref in refs[:count]:
        value = value + ref[...].astype(F32)
    pieces, turned = refs[count:-1], refs[-1]
    value = value.T
    wide = early.shape[0]
    turned[:, :wide] = early[...].astype(F32).T
    turned[:, wide : wide + cols] = value[:, :cols]
    state = value[:, cols : cols + lanes]
    high = state.astype(BF16).astype(F32)
    at = wide + cols
    turned[:, at : at + lanes] = high
    turned[:, at + lanes : at + 2 * lanes] = state - high
    turned[:, at + 2 * lanes :] = value[:, cols + lanes :]
    for k, ref in enumerate(pieces):
        size = ref.shape[0]
        first = pl.multiple_of((part[0] ^ k) * size, 8)
        ref[...] = turned[pl.ds(first, size)].astype(BF16)


def place_kernel(part, *refs):
    pieces = [ref[...].astype(F32) for ref in refs[:WAYS]]
    gate, out, inner, state, step = refs[WAYS:]
    lanes = state.shape[1]
    at = 0
    for result in (gate, out, inner):
        size = result.shape[1] // WAYS
        for k, piece in enumerate(pieces):
            to = pl.multiple_of((part[0] ^ k) * size, LANES)
            result[:, pl.ds(to, size)] = piece[:, at : at + size]
        at += size
    state[...] = sum(piece[:, at : at + lanes] + piece[:, at + lanes : at + 2 * lanes] for piece in pieces)
    at += 2 * lanes
    size = step.shape[1] // WAYS
    for j in range(WAYS):
        value = pieces[0][:, at : at + size]
        for k in range(1, WAYS):
            value = jnp.where((part[0] ^ k) == j, pieces[k][:, at : at + size], value)
        step[:, j * size : (j + 1) * size] = value


def pair_kernel(core, mine, other, base, result):
    same = pl.program_id(0) == core[0]

    @pl.when(same)
    def _():
        result[0] = base[0] + mine[...]

    @pl.when(jnp.logical_not(same))
    def _():
        result[0] = base[0] + other[...]


def pinned(value, near):
    space = pltpu.VMEM if near else pltpu.HBM
    return pltpu.with_memory_space_constraint(value, space)


def result(shape, dtype, near):
    return (pltpu.VMEM if near else pltpu.HBM)(shape, dtype)


def plain_call(body, grid, ins, outs, load, scalars=(), scratch=(), near=(), near_outs=()):
    us, mib = load
    ins = [(pinned(v, i in near), *r) for i, (v, *r) in enumerate(ins)]

    def spec(shape, block, index, once=True):
        if block is None:
            mode = {"pipeline_mode": pl.Buffered(1)} if once and len(shape) > 1 else {}
            return pl.BlockSpec(shape, lambda *a: (0,) * len(shape), **mode)
        return pl.BlockSpec(block, lambda *a: index(*a[: len(grid)]))

    return pl.pallas_call(
        body,
        grid_spec=pltpu.PrefetchScalarGridSpec(
            num_scalar_prefetch=len(scalars),
            grid=grid,
            in_specs=[spec(v.shape, block, index) for v, block, index in ins],
            out_specs=[spec(shape, block, index, False) for shape, _, block, index in outs],
            scratch_shapes=[pltpu.VMEM(shape, dtype) for shape, dtype in scratch],
        ),
        out_shape=[
            result(shape, dtype, i in near_outs) for i, (shape, dtype, _, _) in enumerate(outs)
        ],
        compiler_params=pltpu.CompilerParams(
            dimension_semantics=("arbitrary",) * len(grid), vmem_limit_bytes=mib * MIB
        ),
        cost_estimate=cost_of(us),
    )(*scalars, *[v for v, _, _ in ins])


def whole(value):
    return (value, None, None)


def rows_of(value):
    return (value, (1,) + value.shape[1:], lambda i: (i, 0, 0))


def plane_send(core, own):
    mine = take(own, core[0])
    return [flip(mine, PART, k) for k in range(1, WAYS)]


def gathered_matmul(core, own, near, table, ranges, load, near_outs):
    _, size, depth = own.shape
    far = [flip(value, HEAD, 1) for value in near]
    blocks, step = 2 * WAYS, 2

    def out(cols, dtype):
        return ((blocks, size, cols), dtype, (step, size, cols), lambda i: (i, 0, 0))

    return plain_call(
        functools.partial(gather_kernel, ranges),
        (blocks // step,),
        [whole(v) for v in [own] + near + far + [table]],
        [out(depth, BF16)] + [out(cols, F32) for _, cols in ranges],
        load,
        scalars=(core,),
        near_outs=near_outs,
    )


def token_matmul(tokens, table, columns, load):
    blocks, size, depth = tokens.shape
    cols, step = columns[1], 2
    return plain_call(
        functools.partial(rows_kernel, columns),
        (blocks // step,),
        [(tokens, (step, size, depth), lambda i: (i, 0, 0)), whole(table)],
        [((blocks, size, cols), F32, (step, size, cols), lambda i: (i, 0, 0))],
        load,
        near_outs=(0,),
    )[0]


def to_other_core(lows):
    return [flip(low[WAYS:], HEAD, 1) for low in lows]


def join_matmul(lows, arrived, tables, others, ranges, tokens, load, near, near_outs):
    _, size, _ = lows[0].shape
    depth = tables[0].shape[0]

    def block(v):
        return (v, (2,) + v.shape[1:], lambda i: (i, 0, 0))

    half = (2, size, depth // 2)
    ins = [block(v) for v in lows + arrived] + [whole(t) for t in tables + others]
    outs = [(half, dtype, None, None) for dtype in (F32, F32, BF16, BF16)]
    if tokens is not None:
        ins.append(block(tokens))
        outs.append(((1, depth), F32, None, None))
    return plain_call(
        functools.partial(join_kernel, ranges, tokens is not None),
        (WAYS // 2,),
        ins,
        outs,
        load,
        near=near,
        near_outs=near_outs,
    )


def plane_middle(merged, done, load):
    keep_a, keep_b, send_a, send_b = merged
    keep_a, keep_b = after((keep_a, keep_b), done)
    _, size, half = keep_a.shape
    got_a = flip(send_a, PART, 1)
    got_b = flip(send_b, PART, 2)
    block = (1, size, half)
    sent = plain_call(
        middle_kernel,
        (1,),
        [(v, block, lambda i: (1, 0, 0)) for v in (keep_a, keep_b, got_a, got_b)],
        [((size, half), BF16, None, None)] * 2,
        load,
    )
    return (keep_a, keep_b, got_a, got_b), sent


def plane_sum(parts, sent):
    keep_a, keep_b, got_a, got_b = parts
    a = keep_a[0] + got_a[0].astype(F32) + flip(sent[0], PART, 2).astype(F32)
    b = keep_b[0] + got_b[0].astype(F32) + flip(sent[1], PART, 1).astype(F32)
    return jnp.concatenate([a, b], axis=1)


def pair_add(core, mine, base, load):
    other = flip(mine, HEAD, 1)
    seqs, size, depth = base.shape
    tile = size // 2
    flat = ((tile, depth), lambda i, j: (j, 0))
    deep = ((1, tile, depth), lambda i, j: (i, j, 0))
    return plain_call(
        pair_kernel,
        (seqs, size // tile),
        [(mine, *flat), (other, *flat), (base, *deep)],
        [(base.shape, F32, *deep)],
        load,
        scalars=(core,),
        near=(0, 1),
    )[0]


def after(value, done):
    return lax.optimization_barrier((value, done))[0]


def place_spec(kind, shape, reverse):
    def place(s, b):
        return s * WAYS + (WAYS - 1 - b if reverse else b)

    if kind == ALL:
        return pl.BlockSpec(shape, lambda s, b, o: (0,) * len(shape))
    block = (1,) + tuple(shape[1:])
    if kind == SEQ:
        return pl.BlockSpec(block, lambda s, b, o: (s, 0, 0))
    if kind == PLACE:
        return pl.BlockSpec(block, lambda s, b, o: (place(s, b), 0, 0))
    return pl.BlockSpec(block, lambda s, b, o: (o[place(s, b)], 0, 0))


def block_call(body, order, num_seqs, ins, outs, scratch, reverse, load, near=(), near_outs=()):
    us, mib = load

    ins = [(kind, pinned(v, i in near)) for i, (kind, v) in enumerate(ins)]
    return pl.pallas_call(
        body,
        grid_spec=pltpu.PrefetchScalarGridSpec(
            num_scalar_prefetch=1,
            grid=(num_seqs, WAYS),
            in_specs=[place_spec(kind, v.shape, reverse) for kind, v in ins],
            out_specs=[place_spec(kind, shape, reverse) for kind, shape, _ in outs],
            scratch_shapes=[pltpu.VMEM(shape, dtype) for shape, dtype in scratch],
        ),
        out_shape=[result(shape, dtype, i in near_outs) for i, (_, shape, dtype) in enumerate(outs)],
        compiler_params=pltpu.CompilerParams(
            dimension_semantics=("arbitrary", "arbitrary"), vmem_limit_bytes=mib * MIB
        ),
        cost_estimate=cost_of(us),
    )(order, *[v for _, v in ins])


def per_device(
    hidden,
    norm_gain,
    gate_weight,
    inner_weight,
    state_weight,
    step_weight,
    conv_weight,
    conv_bias,
    state_conv_weight,
    state_conv_bias,
    step_bias,
    log_rate,
    skip_gain,
    out_gain,
    output_projection_weight,
    cotangent,
):
    num_seqs, block_len, model_width = hidden.shape
    planes = lax.axis_size(PLANE)
    rows = gate_weight.shape[0]
    cols = gate_weight.shape[1] // WAYS
    heads = step_bias.shape[0] // WAYS
    width = cols // heads
    state = state_weight.shape[1] // 2
    taps = conv_weight.shape[0]
    inner_total = cols * WAYS * lax.axis_size(HEAD)
    length = WAYS * block_len
    plane = lax.axis_index(PLANE)
    part = lax.axis_index(PART)
    core = lax.axis_index(HEAD)
    core_at = core.astype(jnp.int32)[None]
    blocks = num_seqs * WAYS
    order = jnp.stack(
        [(s ^ core) * WAYS + (b ^ part) for s in range(num_seqs) for b in range(WAYS)]
    ).astype(jnp.int32)
    ring = jnp.arange(WAYS) ^ part

    def my_cols(value, axis, which=None):
        size = value.shape[axis] // WAYS
        at = part if which is None else which
        return lax.dynamic_slice_in_dim(value, at * size, size, axis)

    def pad_heads(value):
        return jnp.pad(value, (0, LANES - heads))[None]

    def to_owner(tables):
        def piece(which):
            return jnp.concatenate([t(which) for t in tables], axis=1)

        got = [piece(part)] + [flip(piece(part ^ k), PART, k) for k in range(1, WAYS)]
        return got[-1], reorder(jnp.stack(got), ring).reshape(WAYS * rows, -1)

    def cut(value):
        return lambda which: my_cols(value, 1, which)

    mixed_cols = cols + 2 * state
    low_state = state_weight.astype(BF16)
    low_step = step_weight.astype(BF16)
    first = mixed_cols + LANES
    arrived, first_rows = to_owner(
        [
            cut(inner_weight.astype(BF16)),
            lambda which: low_state,
            lambda which: jnp.pad(my_cols(low_step, 1, which), ((0, 0), (0, LANES - heads))),
        ]
    )
    inv_rms = lax.rsqrt(jnp.mean(hidden * hidden, axis=-1, keepdims=True) + EPS)
    unit_rows = hidden * inv_rms
    normed = (unit_rows * norm_gain).astype(BF16)
    near = plane_send(core_at, normed)
    in_rows = lax.all_gather(first_rows, PLANE, axis=0, tiled=True)
    later = after((gate_weight, output_projection_weight), near)
    arrived, late_rows = to_owner([cut(later[0].astype(BF16)), cut(later[1].astype(BF16))])
    late_rows = lax.all_gather(late_rows, PLANE, axis=0, tiled=True)
    cot_own = after(cotangent, arrived).astype(BF16)
    cot_near = plane_send(core_at, cot_own)
    tokens, pre, step_raw = gathered_matmul(
        core_at, normed, near, in_rows, [(0, mixed_cols), (mixed_cols, LANES)], (10, 20), ()
    )

    ends = [
        lax.dynamic_slice(
            pre, (order[s * WAYS + WAYS - 1], block_len - 8, 0), (1, 8, mixed_cols)
        )
        for s in range(num_seqs)
    ]
    halo = shift(jnp.concatenate(ends), PLANE, 1)
    taps_all = jnp.concatenate([my_cols(conv_weight, 1), state_conv_weight], axis=1)
    offset = jnp.concatenate([my_cols(conv_bias, 0), state_conv_bias])[None]
    pre_step = step_raw + pad_heads(my_cols(step_bias, 0))
    step_size = jax.nn.softplus(pre_step)
    step_slope = jax.nn.sigmoid(pre_step)
    rate = pad_heads(-jnp.exp(my_cols(log_rate, 0)))
    skip = jnp.repeat(my_cols(skip_gain, 0), width)[None]
    gain = my_cols(out_gain, 0)[None]

    call = functools.partial(block_call, order=order, num_seqs=num_seqs)
    tall = (blocks, block_len, LANES)
    square = (block_len, block_len)
    flat = (blocks, 8, block_len)
    inner = (blocks, block_len, cols)
    states = (blocks, cols, state)
    message = (num_seqs, cols + 8, state)
    act, conv, cum, cum_t, step_t, group_state, leaving = call(
        functools.partial(conv_kernel, width),
        ins=[
            (BLOCK, pre),
            (SEQ, halo),
            (ALL, taps_all),
            (ALL, offset),
            (BLOCK, step_size),
            (ALL, rate),
        ],
        outs=[
            (BLOCK, (blocks, block_len, mixed_cols), F32),
            (BLOCK, (blocks, block_len, mixed_cols), F32),
            (BLOCK, tall, F32),
            (BLOCK, flat, F32),
            (BLOCK, flat, F32),
            (PLACE, states, F32),
            (SEQ, message, F32),
        ],
        scratch=[((block_len + 8, mixed_cols), F32), ((cols, state), F32), ((8, LANES), F32)],
        reverse=False,
        load=(11, 14),
        near_outs=(0, 2),
    )
    came = [shift(leaving, PLANE, 1)]
    (diagonal,) = call(
        functools.partial(diagonal_kernel, width),
        ins=[(BLOCK, act), (BLOCK, cum), (BLOCK, cum_t), (BLOCK, step_t)],
        outs=[(BLOCK, inner, F32)],
        scratch=[(square, F32), ((heads,) + square, BF16)],
        reverse=False,
        load=(5, 14),
        near=(0, 1),
    )
    came.append(shift(after(came[0], diagonal), PLANE, 1))
    gate_pre = token_matmul(after(tokens, came[0]), late_rows, (0, cols), (5, 14))
    came.append(shift(after(came[1], gate_pre), PLANE, 1))
    cot_low, mixed_grad = gathered_matmul(
        core_at, after(cot_own, came[1]), after(cot_near, diagonal), late_rows, [(cols, cols)], (7, 20), (1,)
    )
    for _ in range(4, planes):
        came.append(shift(came[-1], PLANE, 1))
    mixer, incoming, sums = call(
        functools.partial(mixer_kernel, width),
        ins=[
            (BLOCK, act),
            (BLOCK, cum),
            (BLOCK, diagonal),
            (PLACE, group_state),
            (BLOCK, gate_pre),
            (BLOCK, mixed_grad),
            (ALL, skip),
            (ALL, gain),
        ]
        + [(SEQ, v) for v in came],
        outs=[(BLOCK, inner, F32), (PLACE, states, F32), (PLACE, flat, F32)],
        scratch=[((cols, state), F32)],
        reverse=False,
        load=(9, 14),
        near=(0, 1, 4, 5),
        near_outs=(0,),
    )
    sums = total(sums, (HEAD, PART))
    late_other = flip(after(late_rows, sums), HEAD, 1)
    in_other = flip(after(in_rows, late_other), HEAD, 1)
    mixed, mixer_grad, gate_low, state_add, leaving, gain_sum, skip_sum = call(
        functools.partial(gate_kernel, width, inner_total),
        ins=[
            (BLOCK, mixer),
            (BLOCK, gate_pre),
            (BLOCK, mixed_grad),
            (BLOCK, act),
            (BLOCK, cum),
            (PLACE, sums),
            (ALL, gain),
        ],
        outs=[
            (BLOCK, inner, BF16),
            (BLOCK, inner, F32),
            (BLOCK, inner, BF16),
            (PLACE, states, F32),
            (SEQ, message, F32),
            (ALL, (1, cols), F32),
            (ALL, (1, cols), F32),
        ],
        scratch=[((cols, state), F32), ((8, LANES), F32)],
        reverse=True,
        load=(10, 14),
        near=(0, 1, 2, 3, 4),
    )
    came = [shift(leaving, PLANE, -1)]
    mixed_got = to_other_core([mixed])
    deep = WAYS * rows

    group = LANES // math.gcd(deep, LANES)

    def tile(value):
        return (value, (blocks, block_len, group * deep), lambda i: (0, 0, i))

    (early_w,) = plain_call(
        early_grad_kernel,
        (planes // group,),
        [tile(tokens), whole(gate_low), tile(cot_low), whole(mixed)],
        [((planes, 2 * cols, deep), BF16, (group, 2 * cols, deep), lambda i: (i, 0, 0))],
        (9, 24),
        scratch=[((2 * cols, blocks * block_len), BF16)],
    )
    came.append(shift(after(came[0], early_w), PLANE, -1))
    out_merged = join_matmul(
        [mixed], after(mixed_got, came[0]), [late_rows], [late_other], [(cols, cols)], None, (6, 24), (3,), ()
    )
    came.append(shift(after(came[1], out_merged), PLANE, -1))
    for _ in range(4, planes):
        came.append(shift(came[-1], PLANE, -1))
    early_rows = lax.psum_scatter(
        after(early_w, came), PLANE, scatter_dimension=0, tiled=True
    )
    gate_got = to_other_core([gate_low])
    mixer_grad = after(mixer_grad, (out_merged[2:], in_other))
    chan_low, edge, first_rows, taps_sum, bias_sum, rate_sum, step_sum = call(
        functools.partial(back_kernel, width),
        ins=[
            (BLOCK, act),
            (BLOCK, conv),
            (BLOCK, pre),
            (BLOCK, cum),
            (BLOCK, cum_t),
            (BLOCK, step_size),
            (BLOCK, step_t),
            (BLOCK, step_slope),
            (BLOCK, mixer_grad),
            (PLACE, incoming),
            (PLACE, state_add),
            (SEQ, halo),
            (ALL, taps_all),
            (ALL, rate),
            (ALL, skip),
        ]
        + [(SEQ, v) for v in came],
        outs=[
            (BLOCK, (blocks, block_len, first), BF16),
            (SEQ, (num_seqs, EDGE, mixed_cols), F32),
            (SEQ, (num_seqs, 8, mixed_cols), F32),
            (ALL, (8, mixed_cols), F32),
            (ALL, (1, mixed_cols), F32),
            (ALL, (1, LANES), F32),
            (ALL, (1, LANES), F32),
        ],
        scratch=[
            ((cols, state), F32),
            ((block_len + 8, mixed_cols), F32),
            (square, F32),
            ((heads,) + square, BF16),
            (square, F32),
            ((8, block_len), F32),
        ],
        reverse=True,
        load=(28, 22),
        near_outs=(0,),
    )
    following = shift(first_rows, PLANE, -1)
    late = jnp.concatenate([jnp.zeros_like(edge), following], axis=1)
    fix = sum(taps_all[k] * late[:, taps - 1 - k : taps - 1 - k + EDGE] for k in range(taps))
    fixed = after((edge + fix).astype(BF16), early_rows)
    for s in range(num_seqs):
        chan_low = lax.dynamic_update_slice(
            chan_low, fixed[s : s + 1], (order[s * WAYS + WAYS - 1], block_len - EDGE, 0)
        )
    out_parts, out_sent = plane_middle(out_merged, chan_low, (2, 14))
    part_at = part.astype(jnp.int32)[None]

    def exchanged(pieces):
        return [pieces[0]] + [flip(pieces[k], PART, k) for k in range(1, WAYS)]

    chan_low, out_sent, gate_got = lax.optimization_barrier((chan_low, out_sent, gate_got))
    low_got = gate_got + to_other_core([chan_low])
    out_mine = plane_sum(out_parts, out_sent)

    inner_w, state_w, state_other, step_w = plain_call(
        late_grad_kernel,
        (planes // group,),
        [tile(tokens), whole(chan_low)],
        [
            ((planes, c, deep), dtype, (group, c, deep), lambda i: (i, 0, 0))
            for c, dtype in ((cols, BF16), (state, F32), (state, F32), (EDGE, BF16))
        ],
        (9, 22),
        near=(1,),
        scalars=(core_at,),
        scratch=[((first, blocks * block_len), BF16)],
    )
    arrived = flip(state_other, HEAD, 1)
    plane_at = plane.astype(jnp.int32)[None]
    tall = cols + state + EDGE

    def crossed(value):
        block = (1,) + value.shape[1:]
        return pl.BlockSpec(block, lambda k, p: (p[0] ^ k, 0, 0))

    def flat_out(dtype):
        return jax.ShapeDtypeStruct((tall, deep), dtype)

    own_chunk, *sent_chunks = pl.pallas_call(
        chunk_kernel,
        grid_spec=pltpu.PrefetchScalarGridSpec(
            num_scalar_prefetch=1,
            grid=(planes,),
            in_specs=[crossed(v) for v in (inner_w, state_w, arrived, step_w)],
            out_specs=[pl.BlockSpec((tall, deep), lambda k, p: (0, 0))] * planes,
        ),
        out_shape=[flat_out(F32)] + [flat_out(BF16)] * (planes - 1),
        compiler_params=pltpu.CompilerParams(
            dimension_semantics=("arbitrary",), vmem_limit_bytes=8 * MIB
        ),
        cost_estimate=cost_of(3),
    )(plane_at, inner_w, state_w, arrived, step_w)
    got_chunks = [flip(v, PLANE, k + 1) for k, v in enumerate(sent_chunks)]
    *normed_merged, gain_local = join_matmul(
        [after(gate_low, own_chunk), chan_low],
        low_got,
        [late_rows, in_rows],
        [late_other, in_other],
        [(0, cols), (0, first)],
        tokens,
        (11, 30),
        (1, 2, 3, 6, 7),
        (0, 1, 2, 3),
    )
    output = pair_add(core_at, out_mine, hidden, (4, 14))
    keep_a, keep_b, send_a, send_b = normed_merged
    send_a, send_b = after((send_a, send_b), got_chunks[0::2])
    normed_merged = (keep_a, keep_b, send_a, send_b)
    shared = jnp.concatenate(
        [taps_sum[:taps, cols:].reshape(-1), bias_sum[0, cols:], gain_local[0]]
    )
    own = jnp.concatenate(
        [
            taps_sum[:taps, :cols].reshape(-1),
            bias_sum[0, :cols],
            gain_sum[0],
            step_sum[0, :heads],
            rate_sum[0, :heads],
            jnp.sum(skip_sum.reshape(heads, width), axis=1),
        ]
    )
    slots = jnp.where(jnp.arange(WAYS)[:, None] == part, own[None], 0.0)
    shared = total(shared, (HEAD,))
    vector = jnp.concatenate([shared, slots.reshape(-1)])
    normed_parts, normed_sent = plane_middle(
        normed_merged, (got_chunks[1::2], output), (2, 14)
    )
    late_pieces = plain_call(
        functools.partial(turn_kernel, cols, state),
        (1,),
        [whole(v) for v in [early_rows[0], own_chunk] + got_chunks],
        [((rows, 2 * cols + tall + state), BF16, None, None)] * WAYS,
        (3, 16),
        scalars=(part_at,),
        scratch=[((deep, 2 * cols + tall + state), F32)],
    )
    normed_parts = after(normed_parts, late_pieces)
    late_got = exchanged(late_pieces)
    normed_grad = plane_sum(normed_parts, normed_sent)
    unit_mine = take(unit_rows, core)
    unit_grad = normed_grad * norm_gain
    hidden_mine = take(inv_rms, core) * (
        unit_grad - unit_mine * jnp.mean(unit_grad * unit_mine, axis=-1, keepdims=True)
    )
    hidden_grad = pair_add(core_at, hidden_mine, cotangent, (4, 14))
    gate_weight_grad, out_weight_grad, inner_weight_grad, state_mine, step_weight_grad = plain_call(
        place_kernel,
        (1,),
        [whole(v) for v in late_got],
        [
            ((rows, size), F32, None, None)
            for size in (WAYS * cols, WAYS * cols, WAYS * cols, state, WAYS * heads)
        ],
        (4, 16),
        scalars=(part_at,),
    )
    state_weight_grad = jnp.moveaxis(both_cores(state_mine, core), 0, 1).reshape(rows, -1)
    vector = total(after(vector, normed_parts), (PLANE,))
    vector = total(after(vector, hidden_grad), (PART,))
    shared = vector[: shared.shape[0]]
    slots = vector[shared.shape[0] :].reshape(WAYS, -1)
    at = [taps * cols, (taps + 1) * cols, (taps + 2) * cols]
    conv_weight_grad = jnp.moveaxis(slots[:, : at[0]].reshape(WAYS, taps, cols), 0, 1).reshape(
        taps, -1
    )
    conv_bias_grad = slots[:, at[0] : at[1]].reshape(-1)
    out_gain_grad = slots[:, at[1] : at[2]].reshape(-1)
    step_bias_grad = slots[:, at[2] : at[2] + heads].reshape(-1)
    log_rate_grad = slots[:, at[2] + heads : at[2] + 2 * heads].reshape(-1)
    skip_gain_grad = slots[:, at[2] + 2 * heads : at[2] + 3 * heads].reshape(-1)
    state_conv = shared[: (taps + 1) * 2 * state].reshape(taps + 1, 2 * state)
    norm_gain_grad = shared[(taps + 1) * 2 * state :] / norm_gain

    return (
        output,
        hidden_grad,
        norm_gain_grad,
        gate_weight_grad,
        inner_weight_grad,
        state_weight_grad,
        step_weight_grad,
        conv_weight_grad,
        conv_bias_grad,
        state_conv[:taps],
        state_conv[taps],
        step_bias_grad,
        log_rate_grad,
        skip_gain_grad,
        out_gain_grad,
        out_weight_grad,
    )


def solution(mesh):
    grid = mesh.devices
    fine = Mesh(
        grid.reshape(grid.shape[0] // WAYS, WAYS, grid.shape[1]), (PLANE, PART, HEAD)
    )
    seq = (PLANE, PART)
    tokens, table, columns = P(None, seq, None), P(seq, HEAD), P(HEAD)
    return jax.shard_map(
        per_device,
        mesh=fine,
        in_specs=(
            tokens,
            P(),
            table,
            table,
            P(seq, None),
            table,
            P(None, HEAD),
            columns,
            P(),
            P(),
            columns,
            columns,
            columns,
            columns,
            table,
            tokens,
        ),
        out_specs=(
            tokens,
            tokens,
            P(),
            table,
            table,
            P(seq, None),
            table,
            P(None, HEAD),
            columns,
            P(),
            P(),
            columns,
            columns,
            columns,
            columns,
            table,
        ),
        check_vma=False,
    )
```

time: 1730 us -> 425 us (0.25)
  waiting for transfers between devices: 1020 us -> 108 us
  blocking collectives: 215 us -> 0 us
  Pallas kernels: 0 us -> 173 us
  local copies, waits for them, and re-layouts: 180 us -> 32.8 us
  matrix products: 134 us -> 0 us
  other arithmetic: 143 us -> 22.1 us
  starting transfers between devices: 6.34 us -> 65.2 us
    all_gather x5 -> x2, waiting for transfers between devices: 620 us -> 0.01 us  [the longest x1 0.01 us: per_device(): in_rows = lax.all_gather(first_rows, PLANE, axis=0, tiled=True)]
    reduce_scatter x1, waiting for transfers between devices: 223 us -> 2.86 us  [per_device(): lax.psum_scatter(after(early_w, came), PLANE, scatter_dimension=0, tiled=...]
    pallas_call x0 -> x19, Pallas kernels: none -> 173 us  [the longest x13 95.5 us: plain_call(): pl.pallas_call(body, grid_spec=pltpu.PrefetchScalarGridSpec(num_scalar_pr...]
    unnamed x10 -> x3, waiting for transfers between devices: 172 us -> 0.05 us
    dot_general x35 -> x0, matrix products: 134 us -> none  [the longest x1 14.1 us: per_device(): jnp.einsum('rd,rc->dc', columns, flat_proj, preferred_element_type=jnp.fl...]
    all_gather x3 -> x0, blocking collectives: 127 us -> none  [the longest x1 45.4 us: fetch_inputs(): lax.all_gather(state_weight.astype(jnp.bfloat16), 'seq', axis=0, tiled=True)]
    ppermute x2 -> x57, waiting for transfers between devices: 2.82 us -> 105 us  [the longest x49 81.6 us: flip(): return lax.ppermute(value, axis, [(i, i ^ by) for i in range(size)])]
    psum x3 -> x0, blocking collectives: 88.4 us -> none  [the longest x1 83.5 us: per_device(): lax.psum((norm_gain_local, kernel_grad[:, :inner_local], offset_grad[:inn...]
  transfers between devices with their start and end apart: 11 -> 60, of which waited for: 9 -> 23; matrix products, arithmetic and copies ran while one was open for 7% -> 6% of each run, Pallas kernels for 0% -> 38%
where the time goes in v1:
time: 425 us; the launch traced here: 423 us
  Pallas kernels  173 us (41%)
  waiting for transfers between devices  108 us (25%)
  starting transfers between devices  65.2 us (15%)
  local copies, waits for them, and re-layouts  32.8 us (8%)
  between operations  22.4 us (5%)
  other arithmetic  22.1 us (5%)
    pallas_call x13, Pallas kernels, plain_call(): pl.pallas_call(body, grid_spec=pltpu.PrefetchScalarGridSpec(num_scalar_pr...  95.5 us
    ppermute x49, waiting for transfers between devices, flip(): return lax.ppermute(value, axis, [(i, i ^ by) for i in range(size)])  81.6 us
    pallas_call x5, Pallas kernels, block_call(): pl.pallas_call(body, grid_spec=pltpu.PrefetchScalarGridSpec(num_scalar_pr...  74.3 us
    ppermute x49, starting transfers between devices, flip(): return lax.ppermute(value, axis, [(i, i ^ by) for i in range(size)])  41.7 us
    ppermute x8, waiting for transfers between devices, shift(): return lax.ppermute(value, axis, pairs)  23.7 us
    ppermute x8, starting transfers between devices, shift(): return lax.ppermute(value, axis, pairs)  23.4 us
    unnamed x124, local copies, waits for them, and re-layouts  18.9 us
  transfers between devices with their start and end apart: 60, of which 23 were waited for; matrix products, arithmetic and copies ran while one was open for 6% of the time, Pallas kernels for 38%

profile of v1, /device:TPU:0, one launch (start us, length us, event | category | flops | bytes accessed | tf_op | source)
XLA Modules:
  0.0 423.4 jit_solution(13554370789609272729)
XLA Ops:
  32.9 17.0 %collective-permute-done.refs_0_ = bf16[256,1536]{1,0:T(8,128)(2,1)S(1)} collective-permute-done((bf16[256,1536]{1,0:T(8,128)(2,1)S(1)}, bf16[256,1536]{1,0:T(8,128)(2,1)S(1)}, u32[]{:S(2)}, u32[]{:S(2)}) %collective-permute-start) | collective-permute-done | bytes 786464 | tf_op jit(solution)/shard_map/ppermute | solution.py:33
  49.9 16.5 %collective-permute-done.1.refs_1_ = bf16[256,1536]{1,0:T(8,128)(2,1)S(1)} collective-permute-done((bf16[256,1536]{1,0:T(8,128)(2,1)S(1)}, bf16[256,1536]{1,0:T(8,128)(2,1)S(1)}, u32[]{:S(2)}, u32[]{:S(2)}) %collective-permute-start.1) | collective-permute-done | bytes 786464 | tf_op jit(solution)/shard_map/ppermute | solution.py:33
  85.2 13.0 %shard_map.279 = (bf16[8,256,1536]{2,1,0:T(8,128)(2,1)}, f32[8,256,640]{2,1,0:T(8,128)}, f32[8,256,128]{2,1,0:T(8,128)}) custom-call(s32[1]{0:T(128)} %bitcast.core, bf16[2,256,1536]{2,1,0:T(8,128)(2,1)} %copy-done.20, bf16[256,1536]{1,0:T(8,128)(2,1)} %copy-done.27, bf16[256,1536]{1,0:T(8,128)(2,1)} %copy-done.28, ...), custom_call_target="tpu_custom_call" | custom-call | flops 1024 | bytes 35000000 | tf_op jit(solution)/shard_map/pallas_call | solution.py:634
  106.3 14.0 %shard_map.280 = (f32[8,256,640]{2,1,0:T(8,128)S(1)}, f32[8,256,640]{2,1,0:T(8,128)}, f32[8,256,128]{2,1,0:T(8,128)S(1)}, f32[8,8,256]{2,1,0:T(8,128)}, f32[8,8,...) custom-call(s32[8]{0:T(128)S(1)} %stack.93.order, f32[8,256,640]{2,1,0:T(8,128)} %get-tuple-element.110.pre, ...), custom_call_target="tpu_custom_call" | custom-call | flops 1024 | bytes 38500000 | tf_op jit(solution)/shard_map/pallas_call | solution.py:789
  120.4 4.3 %collective-permute-start.10 = (f32[2,392,128]{2,1,0:T(8,128)}, f32[2,392,128]{2,1,0:T(8,128)}, u32[]{:S(2)}, u32[]{:S(2)}) collective-permute-start(f32[2,392,128]{2,1,0:T(8,128)} %get-tuple-element.118), channel_id=1, source_target_pairs={{0,8},{8,16},{16,24},{1,9},{9,17},{17,25},{2,10},{10,18},{18,26},{... | collective-permute-start | bytes 1204232 | tf_op jit(solution)/shard_map/ppermute | solution.py:39
  124.7 9.6 %shard_map.281.diagonal = f32[8,256,384]{2,1,0:T(8,128)} custom-call(s32[8]{0:T(128)S(1)} %stack.93.order, f32[8,256,640]{2,1,0:T(8,128)S(1)} %get-tuple-element.112.act, f32[8,256,128]{2,1,0:T(8,128)S(1)} %get-tuple-element.113.cum, f32[8,8,256]{2,1,0:T(8,128)} %get-tuple-element.114.cum_t, f32[8,8,256]{2,1,0:T(8,128)} %get-tuple-element.115.step_t), custom_call_target="tpu_custom_call" | custom-call | flops 1024 | bytes 17500000 | tf_op jit(solution)/shard_map/pallas_call | solution.py:789
  136.0 5.2 %collective-permute-start.14 = (f32[2,392,128]{2,1,0:T(8,128)}, f32[2,392,128]{2,1,0:T(8,128)}, u32[]{:S(2)}, u32[]{:S(2)}) collective-permute-start(f32[2,392,128]{2,1,0:T(8,128)} %collective-permute-done.10.rest_0_), channel_id=1, source_target_pairs={{0,8},{8,16},{16,24},{1,9},{9,17},{17,25},{2,10},{10,18},{18,26},{... | collective-permute-start | bytes 1204232 | tf_op jit(solution)/shard_map/ppermute | solution.py:39
  141.9 6.6 %shard_map.282.gate = f32[8,256,384]{2,1,0:T(8,128)S(1)} custom-call(bf16[8,256,1536]{2,1,0:T(8,128)(2,1)} %get-tuple-element.119.tokens.refs_8_, bf16[1536,768]{1,0:T(8,128)(2,1)} %all-gather.5.cloned.1.call-done.table.refs_6_.refs_2_.refs_4_), custom_call_target="tpu_custom_call" | custom-call | flops 1024 | bytes 17500000 | tf_op jit(solution)/shard_map/pallas_call | solution.py:634
  149.0 5.2 %collective-permute-start.21 = (f32[2,392,128]{2,1,0:T(8,128)}, f32[2,392,128]{2,1,0:T(8,128)}, u32[]{:S(2)}, u32[]{:S(2)}) collective-permute-start(f32[2,392,128]{2,1,0:T(8,128)} %collective-permute-done.14.rest_1_), channel_id=1, source_target_pairs={{0,8},{8,16},{16,24},{1,9},{9,17},{17,25},{2,10},{10,18},{18,26},{... | collective-permute-start | bytes 1204232 | tf_op jit(solution)/shard_map/ppermute | solution.py:39
  156.3 8.4 %shard_map.283 = (bf16[8,256,1536]{2,1,0:T(8,128)(2,1)}, f32[8,256,384]{2,1,0:T(8,128)S(1)}) custom-call(s32[1]{0:T(128)} %bitcast.core, bf16[2,256,1536]{2,1,0:T(8,128)(2,1)} %copy-done.21, bf16[256,1536]{1,0:T(8,128)(2,1)} %collective-permute-done.15.refs_0_, bf16[256,1536]{1,0:T(8,128)(2,1)} %collective-permute-done.16.refs_1_, ...), custom_call_target="tpu_custom_call" | custom-call | flops 1024 | bytes 24500000 | tf_op jit(solution)/shard_map/pallas_call | solution.py:634
  164.7 9.7 %shard_map.284 = (f32[8,256,384]{2,1,0:T(8,128)S(1)}, f32[8,384,128]{2,1,0:T(8,128)}, f32[8,8,256]{2,1,0:T(8,128)}) custom-call(s32[8]{0:T(128)S(1)} %stack.93.order, f32[8,256,640]{2,1,0:T(8,128)S(1)} %copy-done.3, f32[8,256,128]{2,1,0:T(8,128)S(1)} %copy-done.5, f32[8,256,384]{2,1,0:T(8,128)} %shard_map.281.diagonal, ...), custom_call_target="tpu_custom_call" | custom-call | flops 1024 | bytes 31500000 | tf_op jit(solution)/shard_map/pallas_call | solution.py:789
  186.1 10.9 %shard_map.285 = (bf16[8,256,384]{2,1,0:T(8,128)(2,1)}, f32[8,256,384]{2,1,0:T(8,128)}, bf16[8,256,384]{2,1,0:T(8,128)(2,1)}, f32[8,384,128]{2,1,0:T(8,128)}, f3...) custom-call(s32[8]{0:T(128)S(1)} %stack.93.order, f32[8,256,384]{2,1,0:T(8,128)S(1)} %get-tuple-element.130.mixer, ...), custom_call_target="tpu_custom_call" | custom-call | flops 1024 | bytes 35000000 | tf_op jit(solution)/shard_map/pallas_call | solution.py:789
  200.1 12.2 %shard_map.287 = bf16[4,768,384]{2,1,0:T(8,128)(2,1)} custom-call(bf16[8,256,1536]{2,1,0:T(8,128)(2,1)} %get-tuple-element.119.tokens.refs_8_, bf16[8,256,384]{2,1,0:T(8,128)(2,1)} %get-tuple-element.167.gate_low.refs_0_, bf16[8,256,1536]{2,1,0:T(8,128)(2,1)} %get-tuple-element.147.cot_low, bf16[8,256,384]{2,1,0:T(8,128)(2,1)} %get-tuple-element.132.refs_0_.mixed), custom_call_target="tpu_custom_call" | custom-call | flops 1024 | bytes 31500000 | tf_op jit(solution)/shard_map/pallas_call | solution.py:634
  214.5 8.9 %shard_map.286 = (f32[2,256,768]{2,1,0:T(8,128)}, f32[2,256,768]{2,1,0:T(8,128)}, bf16[2,256,768]{2,1,0:T(8,128)(2,1)}, bf16[2,256,768]{2,1,0:T(8,128)(2,1)}) custom-call(bf16[8,256,384]{2,1,0:T(8,128)(2,1)} %get-tuple-element.132.refs_0_.mixed, bf16[4,256,384]{2,1,0:T(8,128)(2,1)} %copy-done.29, ...), custom_call_target="tpu_custom_call" | custom-call | flops 1024 | bytes 21000000 | tf_op jit(solution)/shard_map/pallas_call | solution.py:634
  228.3 11.7 %collective-permute-done.30.rest_2_ = f32[2,392,128]{2,1,0:T(8,128)} collective-permute-done((f32[2,392,128]{2,1,0:T(8,128)S(1)}, f32[2,392,128]{2,1,0:T(8,128)}, u32[]{:S(2)}, u32[]{:S(2)}) %collective-permute-start.30) | collective-permute-done | bytes 401440 | tf_op jit(solution)/shard_map/ppermute | solution.py:39
  246.3 30.1 %shard_map.288 = (bf16[8,256,768]{2,1,0:T(8,128)(2,1)S(1)}, f32[2,16,640]{2,1,0:T(8,128)}, f32[2,8,640]{2,1,0:T(8,128)}, f32[8,640]{1,0:T(8,128)}, f32[1,640]{1,...) custom-call(s32[8]{0:T(128)S(1)} %stack.93.order, f32[8,256,640]{2,1,0:T(8,128)} %copy-done.2, ...), custom_call_target="tpu_custom_call" | custom-call | flops 1024 | bytes 98000000 | tf_op jit(solution)/shard_map/pallas_call | solution.py:789
  278.0 6.9 %collective-permute-done.31 = f32[2,8,640]{2,1,0:T(8,128)S(1)} collective-permute-done((f32[2,8,640]{2,1,0:T(8,128)}, f32[2,8,640]{2,1,0:T(8,128)S(1)}, u32[]{:S(2)}, u32[]{:S(2)}) %collective-permute-start.31) | collective-permute-done | bytes 40992 | tf_op jit(solution)/shard_map/ppermute | solution.py:39
  294.2 10.0 %shard_map.291 = (bf16[4,384,384]{2,1,0:T(8,128)(2,1)}, f32[4,128,384]{2,1,0:T(8,128)}, f32[4,128,384]{2,1,0:T(8,128)}, bf16[4,16,384]{2,1,0:T(8,128)(2,1)}) custom-call(s32[1]{0:T(128)} %bitcast.core, bf16[8,256,1536]{2,1,0:T(8,128)(2,1)} %get-tuple-element.119.tokens.refs_8_, bf16[8,256,768]{2,1,0:T(8,128)(2,1)S(1)} %slice_dynamic-update-slice_fusion.chan_low.refs_1_), custom_call_target="tpu_custom_call" | custom-call | flops 1024 | bytes 31500000 | tf_op jit(solution)/shard_map/pallas_call | solution.py:634
  319.6 15.3 %shard_map.293 = (f32[2,256,768]{2,1,0:T(8,128)S(1)}, f32[2,256,768]{2,1,0:T(8,128)S(1)}, bf16[2,256,768]{2,1,0:T(8,128)(2,1)}, bf16[2,256,768]{2,1,0:T(8,128)(2,1)}, f32[1,1536]{1,0:T(1,128)}) custom-call(bf16[8,256,384]{2,1,0:T(8,128)(2,1)} %get-tuple-element.167.gate_low.refs_0_, bf16[8,256,768]{2,1,0:T(8,128)(2,1)S(1)} %slice_dynamic-update-slice_fusion.chan_low.refs_1_, ...), custom_call_target="tpu_custom_call" | custom-call | flops 1024 | bytes 38500000 | tf_op jit(solution)/shard_map/pallas_call | solution.py:634
  340.1 5.7 %shard_map.290 = f32[2,256,1536]{2,1,0:T(8,128)} custom-call(s32[1]{0:T(128)} %bitcast.core, f32[256,1536]{1,0:T(8,128)} %pad_maximum_fusion.mine, f32[256,1536]{1,0:T(8,128)} %collective-permute-done.37.other, f32[2,256,1536]{2,1,0:T(8,128)} %base.2), custom_call_target="tpu_custom_call" | custom-call | flops 1024 | bytes 14000000 | tf_op jit(solution)/shard_map/pallas_call | solution.py:634
  345.8 12.5 %collective-permute-done.40.refs_1_ = bf16[528,384]{1,0:T(8,128)(2,1)S(1)} collective-permute-done((bf16[528,384]{1,0:T(8,128)(2,1)}, bf16[528,384]{1,0:T(8,128)(2,1)S(1)}, u32[]{:S(2)}, u32[]{:S(2)}) %collective-permute-start.40) | collective-permute-done | bytes 405536 | tf_op jit(solution)/shard_map/ppermute | solution.py:33
  369.0 4.9 %collective-permute-done.45 = bf16[256,768]{1,0:T(8,128)(2,1)S(1)} collective-permute-done((bf16[256,768]{1,0:T(8,128)(2,1)}, bf16[256,768]{1,0:T(8,128)(2,1)S(1)}, u32[]{:S(2)}, u32[]{:S(2)}) %collective-permute-start.45) | collective-permute-done | bytes 393248 | tf_op jit(solution)/shard_map/ppermute | solution.py:33
  387.7 6.9 %collective-permute-done.54.refs_2_ = bf16[96,1424]{1,0:T(8,128)(2,1)S(1)} collective-permute-done((bf16[96,1424]{1,0:T(8,128)(2,1)}, bf16[96,1424]{1,0:T(8,128)(2,1)S(1)}, u32[]{:S(2)}, u32[]{:S(2)}) %collective-permute-start.54) | collective-permute-done | bytes 273440 | tf_op jit(solution)/shard_map/ppermute | solution.py:33
  398.6 4.4 %shard_map.296 = f32[2,256,1536]{2,1,0:T(8,128)} custom-call(s32[1]{0:T(128)} %bitcast.core, f32[256,1536]{1,0:T(8,128)S(1)} %fusion.2.mine, f32[256,1536]{1,0:T(8,128)S(1)} %collective-permute-done.47.other, f32[2,256,1536]{2,1,0:T(8,128)} %base.3), custom_call_target="tpu_custom_call" | custom-call | flops 1024 | bytes 14000000 | tf_op jit(solution)/shard_map/pallas_call | solution.py:634
  (343 shorter events, 151.2 us)
Async XLA Ops:
  7.2 78.0 %all-gather.3.cloned.1.call-start = ((), (), s32[]{:S(2)}) async-start(), calls=%async_computation.1 | async-start | bytes 2949120 | tf_op jit(solution)/shard_map/all_gather | solution.py:877
  26.5 115.4 %all-gather.5.cloned.1.call-start = ((), (), s32[]{:S(2)}) async-start(), calls=%async_computation.2 | async-start | bytes 2949120 | tf_op jit(solution)/shard_map/all_gather | solution.py:880
  29.3 20.5 %collective-permute-start = (bf16[256,1536]{1,0:T(8,128)(2,1)S(1)}, bf16[256,1536]{1,0:T(8,128)(2,1)S(1)}, u32[]{:S(2)}, u32[]{:S(2)}) collective-permute-start(bf16[256,1536]{1,0:T(8,128)(2,1)S(1)} %dynamic-slice_bitcast_fusion.1), channel_id=1, source_target_pairs={{0,2},{2,0},{4,6},{6,4},{1,3},{3,1},{5,7},{7,5},{8,10},{10,8},{12,... | collective-permute-start | bytes 2359304 | tf_op jit(solution)/shard_map/ppermute | solution.py:33
  31.4 35.0 %collective-permute-start.1 = (bf16[256,1536]{1,0:T(8,128)(2,1)S(1)}, bf16[256,1536]{1,0:T(8,128)(2,1)S(1)}, u32[]{:S(2)}, u32[]{:S(2)}) collective-permute-start(bf16[256,1536]{1,0:T(8,128)(2,1)S(1)} %dynamic-slice_bitcast_fusion.1), channel_id=1, source_target_pairs={{0,4},{2,6},{4,0},{6,2},{1,5},{3,7},{5,1},{7,3},{8,12},{10,14},{12... | collective-permute-start | bytes 2359304 | tf_op jit(solution)/shard_map/ppermute | solution.py:33
  32.9 34.4 %collective-permute-start.2 = (bf16[256,1536]{1,0:T(8,128)(2,1)S(1)}, bf16[256,1536]{1,0:T(8,128)(2,1)}, u32[]{:S(2)}, u32[]{:S(2)}) collective-permute-start(bf16[256,1536]{1,0:T(8,128)(2,1)S(1)} %dynamic-slice_bitcast_fusion.1), channel_id=1, source_target_pairs={{0,6},{2,4},{4,2},{6,0},{1,7},{3,5},{5,3},{7,1},{8,14},{10,12},{12... | collective-permute-start | bytes 2359304 | tf_op jit(solution)/shard_map/ppermute | solution.py:33
  76.9 211.7 %reduce-scatter.2.cloned.1.call-start = ((), (), s32[]{:S(2)}) async-start(), calls=%async_computation.3 | async-start | bytes 2949120 | tf_op jit(solution)/shard_map/reduce_scatter | solution.py:1024
  81.6 59.5 %collective-permute-start.15 = (bf16[256,1536]{1,0:T(8,128)(2,1)S(1)}, bf16[256,1536]{1,0:T(8,128)(2,1)}, u32[]{:S(2)}, u32[]{:S(2)}) collective-permute-start(bf16[256,1536]{1,0:T(8,128)(2,1)S(1)} %dynamic-slice_bitcast_fusion), channel_id=1, source_target_pairs={{0,2},{2,0},{4,6},{6,4},{1,3},{3,1},{5,7},{7,5},{8,10},{10,8},{12,... | collective-permute-start | bytes 2359304 | tf_op jit(solution)/shard_map/ppermute | solution.py:33
  83.2 58.0 %collective-permute-start.16 = (bf16[256,1536]{1,0:T(8,128)(2,1)S(1)}, bf16[256,1536]{1,0:T(8,128)(2,1)}, u32[]{:S(2)}, u32[]{:S(2)}) collective-permute-start(bf16[256,1536]{1,0:T(8,128)(2,1)S(1)} %dynamic-slice_bitcast_fusion), channel_id=1, source_target_pairs={{0,4},{2,6},{4,0},{6,2},{1,5},{3,7},{5,1},{7,3},{8,12},{10,14},{12... | collective-permute-start | bytes 2359304 | tf_op jit(solution)/shard_map/ppermute | solution.py:33
  83.8 57.4 %collective-permute-start.17 = (bf16[256,1536]{1,0:T(8,128)(2,1)S(1)}, bf16[256,1536]{1,0:T(8,128)(2,1)}, u32[]{:S(2)}, u32[]{:S(2)}) collective-permute-start(bf16[256,1536]{1,0:T(8,128)(2,1)S(1)} %dynamic-slice_bitcast_fusion), channel_id=1, source_target_pairs={{0,6},{2,4},{4,2},{6,0},{1,7},{3,5},{5,3},{7,1},{8,14},{10,12},{12... | collective-permute-start | bytes 2359304 | tf_op jit(solution)/shard_map/ppermute | solution.py:33
  120.4 15.7 %collective-permute-start.10 = (f32[2,392,128]{2,1,0:T(8,128)}, f32[2,392,128]{2,1,0:T(8,128)}, u32[]{:S(2)}, u32[]{:S(2)}) collective-permute-start(f32[2,392,128]{2,1,0:T(8,128)} %get-tuple-element.118), channel_id=1, source_target_pairs={{0,8},{8,16},{16,24},{1,9},{9,17},{17,25},{2,10},{10,18},{18,26},{... | collective-permute-start | bytes 1204232 | tf_op jit(solution)/shard_map/ppermute | solution.py:39
  149.0 15.7 %collective-permute-start.21 = (f32[2,392,128]{2,1,0:T(8,128)}, f32[2,392,128]{2,1,0:T(8,128)}, u32[]{:S(2)}, u32[]{:S(2)}) collective-permute-start(f32[2,392,128]{2,1,0:T(8,128)} %collective-permute-done.14.rest_1_), channel_id=1, source_target_pairs={{0,8},{8,16},{16,24},{1,9},{9,17},{17,25},{2,10},{10,18},{18,26},{... | collective-permute-start | bytes 1204232 | tf_op jit(solution)/shard_map/ppermute | solution.py:39
  186.1 27.5 %collective-permute-start.27 = (bf16[1536,768]{1,0:T(8,128)(2,1)}, bf16[1536,768]{1,0:T(8,128)(2,1)}, u32[]{:S(2)}, u32[]{:S(2)}) collective-permute-start(bf16[1536,768]{1,0:T(8,128)(2,1)} %all-gather.5.cloned.1.call-done.table.refs_6_.refs_2_.refs_4_), channel_id=1, source_target_pairs={{0,1},{1,0},{2,3},{3,2},{4,5},{5,4},{6,7},{7,6},{8,9},{9,8},{10,11... | collective-permute-start | bytes 7077896 | tf_op jit(solution)/shard_map/ppermute | solution.py:33
  197.0 15.3 %collective-permute-start.26 = (f32[2,392,128]{2,1,0:T(8,128)}, f32[2,392,128]{2,1,0:T(8,128)S(1)}, u32[]{:S(2)}, u32[]{:S(2)}) collective-permute-start(f32[2,392,128]{2,1,0:T(8,128)} %get-tuple-element.133), channel_id=1, source_target_pairs={{8,0},{16,8},{24,16},{9,1},{17,9},{25,17},{10,2},{18,10},{26,18},{... | collective-permute-start | bytes 1204232 | tf_op jit(solution)/shard_map/ppermute | solution.py:39
  240.1 48.6 %collective-permute-start.32 = (bf16[2,256,768]{2,1,0:T(8,128)(2,1)}, bf16[2,256,768]{2,1,0:T(8,128)(2,1)}, u32[]{:S(2)}, u32[]{:S(2)}) collective-permute-start(bf16[2,256,768]{2,1,0:T(8,128)(2,1)} %get-tuple-element.140), channel_id=1, source_target_pairs={{0,2},{2,0},{4,6},{6,4},{1,3},{3,1},{5,7},{7,5},{8,10},{10,8},{12,... | collective-permute-start | bytes 2359304 | tf_op jit(solution)/shard_map/ppermute | solution.py:33
  241.8 46.9 %collective-permute-start.33 = (bf16[2,256,768]{2,1,0:T(8,128)(2,1)}, bf16[2,256,768]{2,1,0:T(8,128)(2,1)}, u32[]{:S(2)}, u32[]{:S(2)}) collective-permute-start(bf16[2,256,768]{2,1,0:T(8,128)(2,1)} %get-tuple-element.141), channel_id=1, source_target_pairs={{0,4},{2,6},{4,0},{6,2},{1,5},{3,7},{5,1},{7,3},{8,12},{10,14},{12... | collective-permute-start | bytes 2359304 | tf_op jit(solution)/shard_map/ppermute | solution.py:33
  244.2 47.0 %collective-permute-start.34 = (bf16[4,256,384]{2,1,0:T(8,128)(2,1)}, bf16[4,256,384]{2,1,0:T(8,128)(2,1)}, u32[]{:S(2)}, u32[]{:S(2)}) collective-permute-start(bf16[4,256,384]{2,1,0:T(8,128)(2,1)} %slice.152), channel_id=1, source_target_pairs={{0,1},{1,0},{2,3},{3,2},{4,5},{5,4},{6,7},{7,6},{8,9},{9,8},{10,11... | collective-permute-start | bytes 2359304 | tf_op jit(solution)/shard_map/ppermute | solution.py:33
  309.8 30.3 %collective-permute-start.37 = (f32[256,1536]{1,0:T(8,128)}, f32[256,1536]{1,0:T(8,128)}, u32[]{:S(2)}, u32[]{:S(2)}) collective-permute-start(f32[256,1536]{1,0:T(8,128)} %pad_maximum_fusion.mine), channel_id=1, source_target_pairs={{0,1},{1,0},{2,3},{3,2},{4,5},{5,4},{6,7},{7,6},{8,9},{9,8},{10,11... | collective-permute-start | bytes 4718600 | tf_op jit(solution)/shard_map/ppermute | solution.py:33
  316.2 21.0 %collective-permute-start.41 = (bf16[528,384]{1,0:T(8,128)(2,1)S(1)}, bf16[528,384]{1,0:T(8,128)(2,1)S(1)}, u32[]{:S(2)}, u32[]{:S(2)}) collective-permute-start(bf16[528,384]{1,0:T(8,128)(2,1)S(1)} %get-tuple-element.176), channel_id=1, source_target_pairs={{0,8},{8,0},{16,24},{24,16},{1,9},{9,1},{17,25},{25,17},{2,10},{10... | collective-permute-start | bytes 1216520 | tf_op jit(solution)/shard_map/ppermute | solution.py:33
  316.5 21.5 %collective-permute-start.42 = (bf16[528,384]{1,0:T(8,128)(2,1)S(1)}, bf16[528,384]{1,0:T(8,128)(2,1)S(1)}, u32[]{:S(2)}, u32[]{:S(2)}) collective-permute-start(bf16[528,384]{1,0:T(8,128)(2,1)S(1)} %get-tuple-element.177), channel_id=1, source_target_pairs={{0,24},{8,16},{16,8},{24,0},{1,25},{9,17},{17,9},{25,1},{2,26},{10... | collective-permute-start | bytes 1216520 | tf_op jit(solution)/shard_map/ppermute | solution.py:33
  338.0 20.3 %collective-permute-start.43 = (bf16[2,256,768]{2,1,0:T(8,128)(2,1)}, bf16[2,256,768]{2,1,0:T(8,128)(2,1)S(1)}, u32[]{:S(2)}, u32[]{:S(2)}) collective-permute-start(bf16[2,256,768]{2,1,0:T(8,128)(2,1)} %get-tuple-element.178), channel_id=1, source_target_pairs={{0,2},{2,0},{4,6},{6,4},{1,3},{3,1},{5,7},{7,5},{8,10},{10,8},{12,... | collective-permute-start | bytes 2359304 | tf_op jit(solution)/shard_map/ppermute | solution.py:33
  338.8 19.5 %collective-permute-start.44 = (bf16[2,256,768]{2,1,0:T(8,128)(2,1)}, bf16[2,256,768]{2,1,0:T(8,128)(2,1)S(1)}, u32[]{:S(2)}, u32[]{:S(2)}) collective-permute-start(bf16[2,256,768]{2,1,0:T(8,128)(2,1)} %get-tuple-element.179), channel_id=1, source_target_pairs={{0,4},{2,6},{4,0},{6,2},{1,5},{3,7},{5,1},{7,3},{8,12},{10,14},{12... | collective-permute-start | bytes 2359304 | tf_op jit(solution)/shard_map/ppermute | solution.py:33
  339.3 19.0 %collective-permute-start.40 = (bf16[528,384]{1,0:T(8,128)(2,1)}, bf16[528,384]{1,0:T(8,128)(2,1)S(1)}, u32[]{:S(2)}, u32[]{:S(2)}) collective-permute-start(bf16[528,384]{1,0:T(8,128)(2,1)} %get-tuple-element.171), channel_id=1, source_target_pairs={{0,16},{8,24},{16,0},{24,8},{1,17},{9,25},{17,1},{25,9},{2,18},{10... | collective-permute-start | bytes 1216520 | tf_op jit(solution)/shard_map/ppermute | solution.py:33
  376.5 22.0 %collective-permute-start.47 = (f32[256,1536]{1,0:T(8,128)S(1)}, f32[256,1536]{1,0:T(8,128)S(1)}, u32[]{:S(2)}, u32[]{:S(2)}) collective-permute-start(f32[256,1536]{1,0:T(8,128)S(1)} %fusion.2.mine), channel_id=1, source_target_pairs={{0,1},{1,0},{2,3},{3,2},{4,5},{5,4},{6,7},{7,6},{8,9},{9,8},{10,11... | collective-permute-start | bytes 4718600 | tf_op jit(solution)/shard_map/ppermute | solution.py:33
  379.1 15.4 %collective-permute-start.54 = (bf16[96,1424]{1,0:T(8,128)(2,1)}, bf16[96,1424]{1,0:T(8,128)(2,1)S(1)}, u32[]{:S(2)}, u32[]{:S(2)}) collective-permute-start(bf16[96,1424]{1,0:T(8,128)(2,1)} %get-tuple-element.182), channel_id=1, source_target_pairs={{0,4},{2,6},{4,0},{6,2},{1,5},{3,7},{5,1},{7,3},{8,12},{10,14},{12... | collective-permute-start | bytes 820232 | tf_op jit(solution)/shard_map/ppermute | solution.py:33
  (94 other events, 823.4 us)
Sparse Core Ops, SparseCore 0:
  26.6 52.1 all-gather.2
  80.9 49.8 all-gather.4
  240.1 48.4 reduce-scatter.1

commit v2 on v1

--- a/solution.py
+++ b/solution.py
@@ -12,7 +12,6 @@
 WAYS = 4
 LANES = 128
 EDGE = 16
-TILE = 128
 MIB = 1024 * 1024
 PLANE, PART, HEAD = "plane", "part", "head"
 BLOCK, PLACE, SEQ, ALL = range(4)
@@ -54,11 +53,6 @@
 
 def reorder(value, index):
     return jnp.stack([take(value, index[i]) for i in range(value.shape[0])])
-
-
-def both_cores(value, core):
-    other = flip(value, HEAD, 1)
-    return jnp.where(core == 0, jnp.stack([value, other]), jnp.stack([other, value]))
 
 
 def dot(a, b):
@@ -115,6 +109,11 @@
     return sum(dot_nt(part, table) for part in terms_of(value, 2))
 
 
+def to_columns(rows):
+    pad = jnp.zeros((LANES - rows.shape[0], rows.shape[1]), F32)
+    return jnp.concatenate([rows, pad], axis=0).T
+
+
 def pack(leaving, run, run_decay):
     cols = run.shape[0]
     leaving[0, :cols] = run[...]
@@ -131,7 +130,7 @@
             run[at] = ref[0, at] + decay[:, h : h + 1] * run[at]
 
 
-def conv_kernel(width, order, pre, halo, taps, offset, step, rate, act, conv, cum, cum_t, step_t, state, leaving, ext, run, run_decay):
+def conv_kernel(width, order, pre, halo, taps, offset, step, rate, act, conv, cum, cum_t, state, leaving, ext, run, run_decay):
     b = pl.program_id(1)
     size, wide = conv.shape[1:]
     tail_rows = ext.shape[0] - size
@@ -155,11 +154,10 @@
     act[0] = active
     cols = run.shape[0]
     lanes = run.shape[1]
-    steps = step[0]
+    steps = to_columns(step[0])
     total_decay = triangle_sum(size, False, steps * rate[...])
     cum[0] = total_decay
     cum_t[0] = total_decay.T[: cum_t.shape[1]]
-    step_t[0] = steps.T[: cum_t.shape[1]]
     last = total_decay[size - 1 : size]
     tail = spread_heads(jnp.exp(last - total_decay) * steps, head_lanes(cols, width))
     decay = jnp.exp(last)
@@ -173,38 +171,24 @@
     pack(leaving, run, run_decay)
 
 
-def decay_block(column, row, masked):
-    value = column - row
-    if masked:
-        at = lax.broadcasted_iota(jnp.int32, value.shape, 0)
-        value = jnp.where(at >= lax.broadcasted_iota(jnp.int32, value.shape, 1), value, -1e30)
-    return jnp.exp(value)
-
-
-def diagonal_kernel(width, order, act, cum, cum_t, step_t, diagonal, scores, weights):
+def lower(size):
+    row = lax.broadcasted_iota(jnp.int32, (size, size), 0)
+    return row >= lax.broadcasted_iota(jnp.int32, (size, size), 1)
+
+
+def diagonal_kernel(width, order, act, cum, cum_t, step_t, diagonal):
     size, cols = diagonal.shape[1:]
     lanes = (act.shape[2] - cols) // 2
-    heads = cols // width
     low_x = act[0, :, :cols].astype(BF16)
     low_write = act[0, :, cols : cols + lanes].astype(BF16)
     low_read = act[0, :, cols + lanes :].astype(BF16)
-    scores[...] = dot_nt(low_read, low_write)
-
-    @pl.when(jnp.logical_and(pl.program_id(0) == 0, pl.program_id(1) == 0))
-    def _():
-        weights[...] = jnp.zeros_like(weights)
-
-    for h in range(heads):
-        for top in range(0, size, TILE):
-            rows = slice(top, top + TILE)
-            column = cum[0, rows, h : h + 1]
-            for left in range(0, top + TILE, TILE):
-                span = slice(left, left + TILE)
-                table = decay_block(column, cum_t[0, h : h + 1, span], left == top)
-                value = scores[rows, span] * table * step_t[0, h : h + 1, span]
-                weights[h, rows, span] = value.astype(BF16)
+    scores = dot_nt(low_read, low_write)
+    mask = lower(size)
+    for h in range(cols // width):
         at = slice(h * width, (h + 1) * width)
-        diagonal[0, :, at] = dot(weights[h], low_x[:, at])
+        table = jnp.exp(jnp.where(mask, cum[0, :, h : h + 1] - cum_t[0, h : h + 1], -1e30))
+        weights = (scores * table * step_t[0, h : h + 1]).astype(BF16)
+        diagonal[0, :, at] = dot(weights, low_x[:, at])
 
 
 def mixer_kernel(width, order, act, cum, diagonal, state, gate, grad, skip, gain, *rest):
@@ -236,7 +220,7 @@
     sums[0] = both.T[: sums.shape[1]]
 
 
-def gate_kernel(width, inner_total, order, mixer, gate, grad, act, cum, sums, gain, mixed, mixer_grad, gate_low, add, leaving, gain_sum, skip_sum, run, run_decay):
+def gate_kernel(width, inner_total, order, mixer, gate, grad, act, cum, sums, gain, mixed, mixer_grad, gate_low, add, leaving, gain_sum, run, run_decay):
     size, cols = mixed.shape[1:]
     lanes = run.shape[1]
     first = jnp.logical_and(pl.program_id(0) == 0, pl.program_id(1) == 0)
@@ -244,7 +228,6 @@
     @pl.when(first)
     def _():
         gain_sum[...] = jnp.zeros_like(gain_sum)
-        skip_sum[...] = jnp.zeros_like(skip_sum)
 
     @pl.when(pl.program_id(1) == 0)
     def _():
@@ -262,12 +245,12 @@
     scaled = gated * factor
     mixed[0] = (scaled * gain[...]).astype(BF16)
     grads = grad[0]
-    gain_sum[...] += jnp.sum(grads * scaled, axis=0, keepdims=True)
+    gain_sum[0:1] += jnp.sum(grads * scaled, axis=0, keepdims=True)
     gated_grad = factor * (grads * gain[...]) - gated * (factor * factor * factor) * cross
     through = gated_grad * opened
     mixer_grad[0] = through
     gate_low[0] = (gated_grad * value * (sigma * (1.0 + gates * (1.0 - sigma)))).astype(BF16)
-    skip_sum[...] += jnp.sum(through * act[0, :, :cols], axis=0, keepdims=True)
+    gain_sum[1:2] += jnp.sum(through * act[0, :, :cols], axis=0, keepdims=True)
     growth = jnp.exp(cum[0])
     low = through.astype(BF16).astype(F32)
     grown = (low * spread_heads(growth, head_lanes(cols, width))).T
@@ -281,9 +264,9 @@
 
 
 def back_kernel(
-    width, order, act, conv, pre, cum, cum_t, step, step_t, sigma, mixer_grad, incoming, add, halo, taps, rate, skip, *rest
+    width, order, act, conv, pre, cum, cum_t, step_t, sigma, mixer_grad, incoming, add, halo, taps, rate, skip, *rest
 ):
-    *came, chan_low, edge, first_rows, taps_sum, bias_sum, rate_sum, step_sum, run, ext, scores, weights, score_sum, by_col = rest
+    *came, chan_low, edge, first_rows, taps_sum, run, ext = rest
     s, b = pl.program_id(0), pl.program_id(1)
     size, wide = act.shape[1:]
     cols, lanes = run.shape
@@ -292,8 +275,7 @@
 
     @pl.when(jnp.logical_and(s == 0, b == 0))
     def _():
-        for ref in (taps_sum, bias_sum, rate_sum, step_sum):
-            ref[...] = jnp.zeros_like(ref)
+        taps_sum[...] = jnp.zeros_like(taps_sum)
 
     @pl.when(b == 0)
     def _():
@@ -309,7 +291,8 @@
     low_x = active[:, :cols].astype(BF16)
     low_write = active[:, cols : cols + lanes].astype(BF16)
     low_read = active[:, cols + lanes :].astype(BF16)
-    scores[...] = dot_nt(low_read, low_write)
+    scores = dot_nt(low_read, low_write)
+    mask = lower(size)
     outgoing = run[...]
     low_out = outgoing.astype(BF16)
     low_held = incoming[0].astype(BF16)
@@ -318,50 +301,30 @@
     turned = grads.T.astype(BF16)
     decays = cum[0]
     last = decays[size - 1 : size]
-    steps = step[0]
+    steps = to_columns(step_t[0])
     growth = jnp.exp(decays)
     tail_decay = jnp.exp(last - decays)
     tail = tail_decay * steps
     block_decay = jnp.exp(last)
 
-    @pl.when(jnp.logical_and(s == 0, b == 0))
-    def _():
-        weights[...] = jnp.zeros_like(weights)
-        score_sum[...] = jnp.zeros_like(score_sum)
-        by_col[...] = jnp.zeros_like(by_col)
-
-    lane = lax.broadcasted_iota(jnp.int32, (TILE, LANES), 1)
-    row_tiles = [jnp.zeros((TILE, LANES), F32) for _ in range(size // TILE)]
+    lane = lax.broadcasted_iota(jnp.int32, (size, LANES), 1)
+    row8 = lax.broadcasted_iota(jnp.int32, cum_t.shape[1:], 0)
+    by_row = jnp.zeros((size, LANES), F32)
+    by_col = jnp.zeros(cum_t.shape[1:], F32)
+    score_sum = jnp.zeros((size, size), F32)
     pieces = []
     for h in range(heads):
         at = slice(h * width, (h + 1) * width)
         col = slice(h, h + 1)
-        grads_w = dot_nt(low_grad[:, at], low_x[:, at])
-        col_sums = [jnp.zeros((1, TILE), F32) for _ in range(size // TILE)]
-        for i, top in enumerate(range(0, size, TILE)):
-            rows = slice(top, top + TILE)
-            column = decays[rows, col]
-            across = jnp.zeros((TILE, TILE), F32)
-            for j, left in enumerate(range(0, top + TILE, TILE)):
-                span = slice(left, left + TILE)
-                table = decay_block(column, cum_t[0, col, span], left == top)
-                step_row = step_t[0, col, span]
-                score = scores[rows, span]
-                weights[h, rows, span] = (score * table * step_row).astype(BF16)
-                eased = grads_w[rows, span] * table
-                stepped = eased * step_row
-                if h == 0:
-                    score_sum[rows, span] = stepped
-                else:
-                    score_sum[rows, span] += stepped
-                col_sums[j] = col_sums[j] + jnp.sum(eased * score, axis=0, keepdims=True)
-                across = across + stepped * score
-            row_tiles[i] = jnp.where(
-                lane == h, jnp.sum(across, axis=1, keepdims=True), row_tiles[i]
-            )
-        by_col[col] = jnp.concatenate(col_sums, axis=1)
-        pieces.append(dot(turned[at], weights[h]))
-    by_row = jnp.concatenate(row_tiles, axis=0)
+        table = jnp.exp(jnp.where(mask, decays[:, col] - cum_t[0, col], -1e30))
+        step_row = step_t[0, col]
+        weights = (scores * table * step_row).astype(BF16)
+        eased = dot_nt(low_grad[:, at], low_x[:, at]) * table
+        stepped = eased * step_row
+        score_sum = score_sum + stepped
+        by_col = jnp.where(row8 == h, jnp.sum(eased * scores, axis=0, keepdims=True), by_col)
+        by_row = jnp.where(lane == h, jnp.sum(stepped * scores, axis=1, keepdims=True), by_row)
+        pieces.append(dot(turned[at], weights))
 
     table = head_lanes(cols, width)
     tail_all = spread_heads(tail, table)
@@ -370,7 +333,7 @@
     read_held = fine_dot(dot_nt, active[:, cols + lanes :], low_held)
     tail_grad = sum_heads(low_x.astype(F32) * write_out, table)
     read_dot = sum_heads(low_grad.astype(F32) * read_held, table)
-    score_low = score_sum[...].astype(BF16)
+    score_low = score_sum.astype(BF16)
     write_sum = fine_dot(dot, low_x.astype(F32) * tail_all, low_out)
     write_sum = write_sum + dot_tn(score_low, low_read)
     read_sum = fine_dot(dot, low_grad.astype(F32) * growth_all, low_held)
@@ -385,7 +348,7 @@
         run[at] = block_decay[:, col] * outgoing[at] + add[0, at]
 
     pad = jnp.zeros((LANES - by_col.shape[0], size), F32)
-    step_grad = jnp.concatenate([by_col[...], pad], axis=0).T
+    step_grad = jnp.concatenate([by_col, pad], axis=0).T
     tail_through = tail_grad * tail
     row_index = lax.broadcasted_iota(jnp.int32, (size, LANES), 0)
     at_last = jnp.sum(tail_through, axis=0, keepdims=True) + state_dot * block_decay
@@ -393,10 +356,12 @@
     cum_grad = cum_grad + jnp.where(row_index == size - 1, at_last, 0.0)
     rate_grad = triangle_sum(size, True, cum_grad)
     step_grad = step_grad + tail_grad * tail_decay + rate_grad * rate[...]
-    rate_sum[...] += jnp.sum(rate_grad * steps, axis=0, keepdims=True) * rate[...]
-    raw = step_grad * sigma[0]
+    taps_sum[count + 1 : count + 2, LANES : 2 * LANES] += (
+        jnp.sum(rate_grad * steps, axis=0, keepdims=True) * rate[...]
+    )
+    raw = step_grad * to_columns(sigma[0])
     chan_low[0, :, wide:] = raw.astype(BF16)
-    step_sum[...] += jnp.sum(raw, axis=0, keepdims=True)
+    taps_sum[count + 1 : count + 2, :LANES] += jnp.sum(raw, axis=0, keepdims=True)
 
     x_grad = jnp.concatenate(pieces, axis=0).T + write_out * tail_all + skip[...] * grads
     value = conv[0]
@@ -404,7 +369,7 @@
     slope = sig * (1.0 + value * (1.0 - sig))
     conv_grad = jnp.concatenate([x_grad, write_sum, read_sum], axis=1) * slope
     ext[:size] = conv_grad
-    bias_sum[...] += jnp.sum(conv_grad, axis=0, keepdims=True)
+    taps_sum[count : count + 1] += jnp.sum(conv_grad, axis=0, keepdims=True)
     channels = pre[0]
     channel_grad = jnp.zeros((size, wide), F32)
     for k in range(count):
@@ -446,7 +411,13 @@
 
     rows = flat_rows(tokens)
     for (at, size), result in zip(ranges, results):
-        result[...] = dot(rows, table[:, at : at + size]).reshape(result.shape)
+        value = dot(rows, table[:, at : at + size])
+        if result.shape[2] == size:
+            result[...] = value.reshape(result.shape)
+        else:
+            for j in range(step):
+                turned = value[j * result.shape[2] : (j + 1) * result.shape[2]].T
+                result[j] = turned[: result.shape[1]]
 
 
 def rows_kernel(columns, tokens, table, result):
@@ -469,7 +440,10 @@
         def _():
             gain_sum[...] = jnp.zeros_like(gain_sum)
 
-        gain_sum[...] += jnp.sum(value * flat_rows(tokens).astype(F32), axis=0, keepdims=True)
+        sums = jnp.sum(value * flat_rows(tokens).astype(F32), axis=0, keepdims=True)
+        span = gain_sum.shape[1]
+        for r in range(WAYS):
+            gain_sum[r : r + 1] += sums[:, r * span : (r + 1) * span]
     else:
         keep_a, keep_b, send_a, send_b = refs[4 * count :]
     size, half = keep_a.shape[1:]
@@ -557,8 +531,8 @@
             ref[cols + lanes :] = step[0]
 
 
-def turn_kernel(cols, lanes, part, early, own, *refs):
-    count = (len(refs) - 1 - WAYS) if len(refs) > WAYS else 0
+def turn_kernel(cols, lanes, part, small, early, own, *refs):
+    count = len(refs) - 1 - WAYS
     value = own[...]
     for ref in refs[:count]:
         value = value + ref[...].astype(F32)
@@ -573,24 +547,38 @@
     turned[:, at : at + lanes] = high
     turned[:, at + lanes : at + 2 * lanes] = state - high
     turned[:, at + 2 * lanes :] = value[:, cols + lanes :]
+    size = turned.shape[0] // WAYS
+    lines, span = small.shape
+    pad = pieces[0].shape[0] - size
+    sums = small[...]
+    high = sums.astype(BF16).astype(F32)
+    rest = jnp.zeros((lines, turned.shape[1] - 2 * span), F32)
+    sums = jnp.concatenate([high, sums - high, rest], axis=1)
+    below = jnp.zeros((pad - lines, turned.shape[1]), F32)
+    sums = jnp.concatenate([sums, below], axis=0).astype(BF16)
     for k, ref in enumerate(pieces):
-        size = ref.shape[0]
         first = pl.multiple_of((part[0] ^ k) * size, 8)
-        ref[...] = turned[pl.ds(first, size)].astype(BF16)
-
-
-def place_kernel(part, *refs):
-    pieces = [ref[...].astype(F32) for ref in refs[:WAYS]]
-    gate, out, inner, state, step = refs[WAYS:]
-    lanes = state.shape[1]
+        ref[:pad] = sums
+        ref[pad:] = turned[pl.ds(first, size)].astype(BF16)
+
+
+def place_kernel(span, part, *refs):
+    gate, out, inner, final, step, convs, bias, gains, heads = refs[WAYS:]
+    rows, lanes = gate.shape[0], final.shape[1]
+    cols = gate.shape[1] // WAYS
+    values = [ref[...].astype(F32) for ref in refs[:WAYS]]
+    pad = values[0].shape[0] - rows
+    pieces = [value[pad:] for value in values]
+    sums = [value[:24, :span] + value[:24, span : 2 * span] for value in values]
     at = 0
     for result in (gate, out, inner):
-        size = result.shape[1] // WAYS
         for k, piece in enumerate(pieces):
-            to = pl.multiple_of((part[0] ^ k) * size, LANES)
-            result[:, pl.ds(to, size)] = piece[:, at : at + size]
-        at += size
-    state[...] = sum(piece[:, at : at + lanes] + piece[:, at + lanes : at + 2 * lanes] for piece in pieces)
+            to = pl.multiple_of((part[0] ^ k) * cols, LANES)
+            result[:, pl.ds(to, cols)] = piece[:, at : at + cols]
+        at += cols
+    final[:rows] = sum(
+        piece[:, at : at + lanes] + piece[:, at + lanes : at + 2 * lanes] for piece in pieces
+    )
     at += 2 * lanes
     size = step.shape[1] // WAYS
     for j in range(WAYS):
@@ -598,6 +586,26 @@
         for k in range(1, WAYS):
             value = jnp.where((part[0] ^ k) == j, pieces[k][:, at : at + size], value)
         step[:, j * size : (j + 1) * size] = value
+    shared = sum(sums)
+    lines = [shared[i : i + 1, cols + j * lanes : cols + (j + 1) * lanes] for i in range(5) for j in range(2)]
+    lines += [
+        shared[16 + r : 17 + r, j * lanes : (j + 1) * lanes]
+        for r in range(WAYS)
+        for j in range(cols // lanes)
+    ]
+    for i, line in enumerate(lines):
+        final[rows + i : rows + i + 1] = line
+    left = final.shape[0] - rows - len(lines)
+    final[rows + len(lines) :] = jnp.zeros((left, lanes), F32)
+    for k, value in enumerate(sums):
+        to = pl.multiple_of((part[0] ^ k) * cols, LANES)
+        count = convs.shape[0]
+        convs[:, pl.ds(to, cols)] = value[:count, :cols]
+        bias[:, pl.ds(to, cols)] = value[count : count + 1, :cols]
+        gains[:, pl.ds(to, cols)] = value[8:9, :cols]
+        skips = sum_heads(value[8:16, :cols], head_lanes(cols, cols // size))
+        slot = pl.ds(part[0] ^ k, 1)
+        heads[slot] = jnp.concatenate([value[count + 1 : count + 2, : 2 * LANES], skips[1:2]], axis=1)
 
 
 def pair_kernel(core, mine, other, base, result):
@@ -671,11 +679,13 @@
     def out(cols, dtype):
         return ((blocks, size, cols), dtype, (step, size, cols), lambda i: (i, 0, 0))
 
+    rows_out = ((blocks, 8, size), F32, (step, 8, size), lambda i: (i, 0, 0))
     return plain_call(
         functools.partial(gather_kernel, ranges),
         (blocks // step,),
         [whole(v) for v in [own] + near + far + [table]],
-        [out(depth, BF16)] + [out(cols, F32) for _, cols in ranges],
+        [out(depth, BF16)]
+        + [out(cols, F32) if cols > LANES else rows_out for _, cols in ranges],
         load,
         scalars=(core,),
         near_outs=near_outs,
@@ -711,7 +721,7 @@
     outs = [(half, dtype, None, None) for dtype in (F32, F32, BF16, BF16)]
     if tokens is not None:
         ins.append(block(tokens))
-        outs.append(((1, depth), F32, None, None))
+        outs.append(((8, depth // WAYS), F32, None, None))
     return plain_call(
         functools.partial(join_kernel, ranges, tokens is not None),
         (WAYS // 2,),
@@ -893,7 +903,7 @@
     halo = shift(jnp.concatenate(ends), PLANE, 1)
     taps_all = jnp.concatenate([my_cols(conv_weight, 1), state_conv_weight], axis=1)
     offset = jnp.concatenate([my_cols(conv_bias, 0), state_conv_bias])[None]
-    pre_step = step_raw + pad_heads(my_cols(step_bias, 0))
+    pre_step = step_raw + jnp.pad(my_cols(step_bias, 0), (0, 8 - heads))[:, None]
     step_size = jax.nn.softplus(pre_step)
     step_slope = jax.nn.sigmoid(pre_step)
     rate = pad_heads(-jnp.exp(my_cols(log_rate, 0)))
@@ -902,12 +912,11 @@
 
     call = functools.partial(block_call, order=order, num_seqs=num_seqs)
     tall = (blocks, block_len, LANES)
-    square = (block_len, block_len)
     flat = (blocks, 8, block_len)
     inner = (blocks, block_len, cols)
     states = (blocks, cols, state)
     message = (num_seqs, cols + 8, state)
-    act, conv, cum, cum_t, step_t, group_state, leaving = call(
+    act, conv, cum, cum_t, group_state, leaving = call(
         functools.partial(conv_kernel, width),
         ins=[
             (BLOCK, pre),
@@ -922,7 +931,6 @@
             (BLOCK, (blocks, block_len, mixed_cols), F32),
             (BLOCK, tall, F32),
             (BLOCK, flat, F32),
-            (BLOCK, flat, F32),
             (PLACE, states, F32),
             (SEQ, message, F32),
         ],
@@ -934,9 +942,9 @@
     came = [shift(leaving, PLANE, 1)]
     (diagonal,) = call(
         functools.partial(diagonal_kernel, width),
-        ins=[(BLOCK, act), (BLOCK, cum), (BLOCK, cum_t), (BLOCK, step_t)],
+        ins=[(BLOCK, act), (BLOCK, cum), (BLOCK, cum_t), (BLOCK, step_size)],
         outs=[(BLOCK, inner, F32)],
-        scratch=[(square, F32), ((heads,) + square, BF16)],
+        scratch=[],
         reverse=False,
         load=(5, 14),
         near=(0, 1),
@@ -972,7 +980,7 @@
     sums = total(sums, (HEAD, PART))
     late_other = flip(after(late_rows, sums), HEAD, 1)
     in_other = flip(after(in_rows, late_other), HEAD, 1)
-    mixed, mixer_grad, gate_low, state_add, leaving, gain_sum, skip_sum = call(
+    mixed, mixer_grad, gate_low, state_add, leaving, gain_sum = call(
         functools.partial(gate_kernel, width, inner_total),
         ins=[
             (BLOCK, mixer),
@@ -989,8 +997,7 @@
             (BLOCK, inner, BF16),
             (PLACE, states, F32),
             (SEQ, message, F32),
-            (ALL, (1, cols), F32),
-            (ALL, (1, cols), F32),
+            (ALL, (8, cols), F32),
         ],
         scratch=[((cols, state), F32), ((8, LANES), F32)],
         reverse=True,
@@ -1026,7 +1033,7 @@
     )
     gate_got = to_other_core([gate_low])
     mixer_grad = after(mixer_grad, (out_merged[2:], in_other))
-    chan_low, edge, first_rows, taps_sum, bias_sum, rate_sum, step_sum = call(
+    chan_low, edge, first_rows, taps_sum = call(
         functools.partial(back_kernel, width),
         ins=[
             (BLOCK, act),
@@ -1035,7 +1042,6 @@
             (BLOCK, cum),
             (BLOCK, cum_t),
             (BLOCK, step_size),
-            (BLOCK, step_t),
             (BLOCK, step_slope),
             (BLOCK, mixer_grad),
             (PLACE, incoming),
@@ -1051,17 +1057,10 @@
             (SEQ, (num_seqs, EDGE, mixed_cols), F32),
             (SEQ, (num_seqs, 8, mixed_cols), F32),
             (ALL, (8, mixed_cols), F32),
-            (ALL, (1, mixed_cols), F32),
-            (ALL, (1, LANES), F32),
-            (ALL, (1, LANES), F32),
         ],
         scratch=[
             ((cols, state), F32),
             ((block_len + 8, mixed_cols), F32),
-            (square, F32),
-            ((heads,) + square, BF16),
-            (square, F32),
-            ((8, block_len), F32),
         ],
         reverse=True,
         load=(28, 22),
@@ -1107,7 +1106,7 @@
         return pl.BlockSpec(block, lambda k, p: (p[0] ^ k, 0, 0))
 
     def flat_out(dtype):
-        return jax.ShapeDtypeStruct((tall, deep), dtype)
+        return result((tall, deep), dtype, False)
 
     own_chunk, *sent_chunks = pl.pallas_call(
         chunk_kernel,
@@ -1122,7 +1121,7 @@
             dimension_semantics=("arbitrary",), vmem_limit_bytes=8 * MIB
         ),
         cost_estimate=cost_of(3),
-    )(plane_at, inner_w, state_w, arrived, step_w)
+    )(plane_at, *[pinned(v, False) for v in (inner_w, state_w, arrived, step_w)])
     got_chunks = [flip(v, PLANE, k + 1) for k, v in enumerate(sent_chunks)]
     *normed_merged, gain_local = join_matmul(
         [after(gate_low, own_chunk), chan_low],
@@ -1139,36 +1138,24 @@
     keep_a, keep_b, send_a, send_b = normed_merged
     send_a, send_b = after((send_a, send_b), got_chunks[0::2])
     normed_merged = (keep_a, keep_b, send_a, send_b)
-    shared = jnp.concatenate(
-        [taps_sum[:taps, cols:].reshape(-1), bias_sum[0, cols:], gain_local[0]]
-    )
-    own = jnp.concatenate(
-        [
-            taps_sum[:taps, :cols].reshape(-1),
-            bias_sum[0, :cols],
-            gain_sum[0],
-            step_sum[0, :heads],
-            rate_sum[0, :heads],
-            jnp.sum(skip_sum.reshape(heads, width), axis=1),
-        ]
-    )
-    slots = jnp.where(jnp.arange(WAYS)[:, None] == part, own[None], 0.0)
-    shared = total(shared, (HEAD,))
-    vector = jnp.concatenate([shared, slots.reshape(-1)])
+    wide_pad = ((0, 0), (0, mixed_cols - cols))
+    vector = jnp.concatenate([taps_sum, jnp.pad(gain_sum, wide_pad), jnp.pad(gain_local, wide_pad)])
     normed_parts, normed_sent = plane_middle(
         normed_merged, (got_chunks[1::2], output), (2, 14)
     )
+    vector = total(vector, (PLANE,))
+    line = 2 * cols + tall + state
+    extra = -(-vector.shape[0] // EDGE) * EDGE
     late_pieces = plain_call(
         functools.partial(turn_kernel, cols, state),
         (1,),
-        [whole(v) for v in [early_rows[0], own_chunk] + got_chunks],
-        [((rows, 2 * cols + tall + state), BF16, None, None)] * WAYS,
-        (3, 16),
+        [whole(v) for v in [vector, early_rows[0], own_chunk] + got_chunks],
+        [((rows + extra, line), BF16, None, None)] * WAYS,
+        (3, 18),
         scalars=(part_at,),
-        scratch=[((deep, 2 * cols + tall + state), F32)],
+        scratch=[((deep, line), F32)],
     )
     normed_parts = after(normed_parts, late_pieces)
-    late_got = exchanged(late_pieces)
     normed_grad = plane_sum(normed_parts, normed_sent)
     unit_mine = take(unit_rows, core)
     unit_grad = normed_grad * norm_gain
@@ -1176,34 +1163,45 @@
         unit_grad - unit_mine * jnp.mean(unit_grad * unit_mine, axis=-1, keepdims=True)
     )
     hidden_grad = pair_add(core_at, hidden_mine, cotangent, (4, 14))
-    gate_weight_grad, out_weight_grad, inner_weight_grad, state_mine, step_weight_grad = plain_call(
-        place_kernel,
+    late_got = exchanged([*late_pieces[:-1], after(late_pieces[-1], hidden_grad)])
+    lines = 2 * (taps + 1) + model_width // state + 2
+    sizes = (
+        (rows, WAYS * cols),
+        (rows, WAYS * cols),
+        (rows, WAYS * cols),
+        (rows + lines, state),
+        (rows, WAYS * heads),
+        (taps, WAYS * cols),
+        (1, WAYS * cols),
+        (1, WAYS * cols),
+        (WAYS, 3 * LANES),
+    )
+    placed = plain_call(
+        functools.partial(place_kernel, mixed_cols),
         (1,),
         [whole(v) for v in late_got],
+        [(shape, F32, None, None) for shape in sizes],
+        (4, 20),
+        scalars=(part_at,),
+    )
+    gate_weight_grad, out_weight_grad, inner_weight_grad, final, step_weight_grad = placed[:5]
+    conv_weight_grad, conv_bias_grad, out_gain_grad, by_head = placed[5:]
+    other = flip(final, HEAD, 1)
+    mine_first = core == 0
+    state_weight_grad = jnp.concatenate(
         [
-            ((rows, size), F32, None, None)
-            for size in (WAYS * cols, WAYS * cols, WAYS * cols, state, WAYS * heads)
+            jnp.where(mine_first, final[:rows], other[:rows]),
+            jnp.where(mine_first, other[:rows], final[:rows]),
         ],
-        (4, 16),
-        scalars=(part_at,),
-    )
-    state_weight_grad = jnp.moveaxis(both_cores(state_mine, core), 0, 1).reshape(rows, -1)
-    vector = total(after(vector, normed_parts), (PLANE,))
-    vector = total(after(vector, hidden_grad), (PART,))
-    shared = vector[: shared.shape[0]]
-    slots = vector[shared.shape[0] :].reshape(WAYS, -1)
-    at = [taps * cols, (taps + 1) * cols, (taps + 2) * cols]
-    conv_weight_grad = jnp.moveaxis(slots[:, : at[0]].reshape(WAYS, taps, cols), 0, 1).reshape(
-        taps, -1
-    )
-    conv_bias_grad = slots[:, at[0] : at[1]].reshape(-1)
-    out_gain_grad = slots[:, at[1] : at[2]].reshape(-1)
-    step_bias_grad = slots[:, at[2] : at[2] + heads].reshape(-1)
-    log_rate_grad = slots[:, at[2] + heads : at[2] + 2 * heads].reshape(-1)
-    skip_gain_grad = slots[:, at[2] + 2 * heads : at[2] + 3 * heads].reshape(-1)
-    state_conv = shared[: (taps + 1) * 2 * state].reshape(taps + 1, 2 * state)
-    norm_gain_grad = shared[(taps + 1) * 2 * state :] / norm_gain
-
+        axis=1,
+    )
+    shared = final[rows:] + other[rows:]
+    state_conv = shared[: 2 * (taps + 1)].reshape(taps + 1, 2 * state)
+    norm_gain_grad = shared[2 * (taps + 1) : lines - 2].reshape(-1) / norm_gain
+    conv_bias_grad = conv_bias_grad[0]
+    out_gain_grad = out_gain_grad[0]
+    by_head = by_head.reshape(WAYS, 3, LANES)[:, :, :heads]
+    step_bias_grad, log_rate_grad, skip_gain_grad = [by_head[:, i].reshape(-1) for i in range(3)]
     return (
         output,
         hidden_grad,

time: 425 us -> 419 us (0.986)
  local copies, waits for them, and re-layouts: 32.8 us -> 27 us
    ppermute x49 -> x46, waiting for transfers between devices: 81.6 us -> 75.5 us  [flip(): return lax.ppermute(value, axis, [(i, i ^ by) for i in range(size)])]
    unnamed x124 -> x109, local copies, waits for them, and re-layouts: 18.9 us -> 14 us
    ppermute x49 -> x46, starting transfers between devices: 41.7 us -> 41.2 us  [flip(): return lax.ppermute(value, axis, [(i, i ^ by) for i in range(size)])]
  transfers between devices with their start and end apart: 60 -> 57, of which waited for: 23 -> 24; matrix products, arithmetic and copies ran while one was open for 6% -> 7% of each run, Pallas kernels for 38% -> 38%
where the time goes in v2:
time: 419 us; the launch traced here: 417 us
  Pallas kernels  171 us (41%)
  waiting for transfers between devices  105 us (25%)
  starting transfers between devices  65.8 us (16%)
  local copies, waits for them, and re-layouts  27 us (6%)
  other arithmetic  25.5 us (6%)
  between operations  22.2 us (5%)
    pallas_call x13, Pallas kernels, plain_call(): pl.pallas_call(body, grid_spec=pltpu.PrefetchScalarGridSpec(num_scalar_pr...  95 us
    ppermute x46, waiting for transfers between devices, flip(): return lax.ppermute(value, axis, [(i, i ^ by) for i in range(size)])  75.5 us
    pallas_call x5, Pallas kernels, block_call(): pl.pallas_call(body, grid_spec=pltpu.PrefetchScalarGridSpec(num_scalar_pr...  72.3 us
    ppermute x46, starting transfers between devices, flip(): return lax.ppermute(value, axis, [(i, i ^ by) for i in range(size)])  41.2 us
    ppermute x8, waiting for transfers between devices, shift(): return lax.ppermute(value, axis, pairs)  25.3 us
    ppermute x8, starting transfers between devices, shift(): return lax.ppermute(value, axis, pairs)  24.5 us
    unnamed x109, local copies, waits for them, and re-layouts  14 us
  transfers between devices with their start and end apart: 57, of which 24 were waited for; matrix products, arithmetic and copies ran while one was open for 7% of the time, Pallas kernels for 38%

profile of v2, /device:TPU:0, one launch (start us, length us, event | category | flops | bytes accessed | tf_op | source)
XLA Modules:
  0.0 416.9 jit_solution(11404668277876897514)
XLA Ops:
  32.9 17.0 %collective-permute-done.refs_0_ = bf16[256,1536]{1,0:T(8,128)(2,1)S(1)} collective-permute-done((bf16[256,1536]{1,0:T(8,128)(2,1)S(1)}, bf16[256,1536]{1,0:T(8,128)(2,1)S(1)}, u32[]{:S(2)}, u32[]{:S(2)}) %collective-permute-start) | collective-permute-done | bytes 786464 | tf_op jit(solution)/shard_map/ppermute | solution.py:32
  49.9 16.5 %collective-permute-done.1.refs_1_ = bf16[256,1536]{1,0:T(8,128)(2,1)S(1)} collective-permute-done((bf16[256,1536]{1,0:T(8,128)(2,1)S(1)}, bf16[256,1536]{1,0:T(8,128)(2,1)S(1)}, u32[]{:S(2)}, u32[]{:S(2)}) %collective-permute-start.1) | collective-permute-done | bytes 786464 | tf_op jit(solution)/shard_map/ppermute | solution.py:32
  85.2 12.9 %shard_map.279 = (bf16[8,256,1536]{2,1,0:T(8,128)(2,1)}, f32[8,256,640]{2,1,0:T(8,128)}, f32[8,8,256]{2,1,0:T(8,128)}) custom-call(s32[1]{0:T(128)} %bitcast.core, bf16[2,256,1536]{2,1,0:T(8,128)(2,1)} %copy-done.16, bf16[256,1536]{1,0:T(8,128)(2,1)} %copy-done.23, bf16[256,1536]{1,0:T(8,128)(2,1)} %copy-done.24, ...), custom_call_target="tpu_custom_call" | custom-call | flops 1024 | bytes 35000000 | tf_op jit(solution)/shard_map/pallas_call | solution.py:642
  105.3 14.8 %shard_map.280 = (f32[8,256,640]{2,1,0:T(8,128)S(1)}, f32[8,256,640]{2,1,0:T(8,128)}, f32[8,256,128]{2,1,0:T(8,128)S(1)}, f32[8,8,256]{2,1,0:T(8,128)}, f32[8,384,128]{2,1,0:T(8,128)}, /*index=5*/f32[2,392,128]{2,1,0:T(8,128)}) custom-call(s32[8]{0:T(128)S(1)} %stack.79.order, f32[8,256,640]{2,1,0:T(8,128)} %get-tuple-element.108.pre, ...), custom_call_target="tpu_custom_call" | custom-call | flops 1024 | bytes 38500000 | tf_op jit(solution)/shard_map/pallas_call | solution.py:799
  120.2 5.2 %collective-permute-start.10 = (f32[2,392,128]{2,1,0:T(8,128)}, f32[2,392,128]{2,1,0:T(8,128)}, u32[]{:S(2)}, u32[]{:S(2)}) collective-permute-start(f32[2,392,128]{2,1,0:T(8,128)} %get-tuple-element.115), channel_id=1, source_target_pairs={{0,8},{8,16},{16,24},{1,9},{9,17},{17,25},{2,10},{10,18},{18,26},{... | collective-permute-start | bytes 1204232 | tf_op jit(solution)/shard_map/ppermute | solution.py:38
  125.4 7.9 %shard_map.281.diagonal = f32[8,256,384]{2,1,0:T(8,128)} custom-call(s32[8]{0:T(128)S(1)} %stack.79.order, f32[8,256,640]{2,1,0:T(8,128)S(1)} %get-tuple-element.110.act, f32[8,256,128]{2,1,0:T(8,128)S(1)} %get-tuple-element.111.cum, f32[8,8,256]{2,1,0:T(8,128)} %get-tuple-element.112.cum_t, f32[8,8,256]{2,1,0:T(8,128)} %get-tuple-element.263.step.step_t), custom_call_target="tpu_custom_call" | custom-call | flops 1024 | bytes 17500000 | tf_op jit(solution)/shard_map/pallas_call | solution.py:799
  136.0 5.2 %collective-permute-start.14 = (f32[2,392,128]{2,1,0:T(8,128)}, f32[2,392,128]{2,1,0:T(8,128)}, u32[]{:S(2)}, u32[]{:S(2)}) collective-permute-start(f32[2,392,128]{2,1,0:T(8,128)} %collective-permute-done.10.rest_0_), channel_id=1, source_target_pairs={{0,8},{8,16},{16,24},{1,9},{9,17},{17,25},{2,10},{10,18},{18,26},{... | collective-permute-start | bytes 1204232 | tf_op jit(solution)/shard_map/ppermute | solution.py:38
  141.9 6.6 %shard_map.282.gate = f32[8,256,384]{2,1,0:T(8,128)S(1)} custom-call(bf16[8,256,1536]{2,1,0:T(8,128)(2,1)} %get-tuple-element.116.tokens.refs_8_, bf16[1536,768]{1,0:T(8,128)(2,1)} %all-gather.5.cloned.1.call-done.table.refs_6_.refs_2_.refs_4_), custom_call_target="tpu_custom_call" | custom-call | flops 1024 | bytes 17500000 | tf_op jit(solution)/shard_map/pallas_call | solution.py:642
  148.8 5.2 %collective-permute-start.21 = (f32[2,392,128]{2,1,0:T(8,128)}, f32[2,392,128]{2,1,0:T(8,128)}, u32[]{:S(2)}, u32[]{:S(2)}) collective-permute-start(f32[2,392,128]{2,1,0:T(8,128)} %collective-permute-done.14.rest_1_), channel_id=1, source_target_pairs={{0,8},{8,16},{16,24},{1,9},{9,17},{17,25},{2,10},{10,18},{18,26},{... | collective-permute-start | bytes 1204232 | tf_op jit(solution)/shard_map/ppermute | solution.py:38
  156.1 8.4 %shard_map.283 = (bf16[8,256,1536]{2,1,0:T(8,128)(2,1)}, f32[8,256,384]{2,1,0:T(8,128)S(1)}) custom-call(s32[1]{0:T(128)} %bitcast.core, bf16[2,256,1536]{2,1,0:T(8,128)(2,1)} %copy-done.17, bf16[256,1536]{1,0:T(8,128)(2,1)} %collective-permute-done.15.refs_0_, bf16[256,1536]{1,0:T(8,128)(2,1)} %collective-permute-done.16.refs_1_, ...), custom_call_target="tpu_custom_call" | custom-call | flops 1024 | bytes 24500000 | tf_op jit(solution)/shard_map/pallas_call | solution.py:642
  164.6 9.7 %shard_map.284 = (f32[8,256,384]{2,1,0:T(8,128)S(1)}, f32[8,384,128]{2,1,0:T(8,128)}, f32[8,8,256]{2,1,0:T(8,128)}) custom-call(s32[8]{0:T(128)S(1)} %stack.79.order, f32[8,256,640]{2,1,0:T(8,128)S(1)} %copy-done.3, f32[8,256,128]{2,1,0:T(8,128)S(1)} %copy-done.5, f32[8,256,384]{2,1,0:T(8,128)} %shard_map.281.diagonal, ...), custom_call_target="tpu_custom_call" | custom-call | flops 1024 | bytes 31500000 | tf_op jit(solution)/shard_map/pallas_call | solution.py:799
  185.9 10.9 %shard_map.285 = (bf16[8,256,384]{2,1,0:T(8,128)(2,1)}, f32[8,256,384]{2,1,0:T(8,128)}, bf16[8,256,384]{2,1,0:T(8,128)(2,1)}, f32[8,384,128]{2,1,0:T(8,128)}, f32[2,392,128]{2,1,0:T(8,128)}, /*index=5*/f32[8,384]{1,0:T(8,128)}) custom-call(s32[8]{0:T(128)S(1)} %stack.79.order, f32[8,256,384]{2,1,0:T(8,128)S(1)} %get-tuple-element.127.mixer, ...), custom_call_target="tpu_custom_call" | custom-call | flops 1024 | bytes 35000000 | tf_op jit(solution)/shard_map/pallas_call | solution.py:799
  200.1 12.2 %shard_map.287 = bf16[4,768,384]{2,1,0:T(8,128)(2,1)} custom-call(bf16[8,256,1536]{2,1,0:T(8,128)(2,1)} %get-tuple-element.116.tokens.refs_8_, bf16[8,256,384]{2,1,0:T(8,128)(2,1)} %get-tuple-element.164.gate_low.refs_0_, bf16[8,256,1536]{2,1,0:T(8,128)(2,1)} %get-tuple-element.144.cot_low, bf16[8,256,384]{2,1,0:T(8,128)(2,1)} %get-tuple-element.129.refs_0_.mixed), custom_call_target="tpu_custom_call" | custom-call | flops 1024 | bytes 31500000 | tf_op jit(solution)/shard_map/pallas_call | solution.py:642
  214.5 8.9 %shard_map.286 = (f32[2,256,768]{2,1,0:T(8,128)}, f32[2,256,768]{2,1,0:T(8,128)}, bf16[2,256,768]{2,1,0:T(8,128)(2,1)}, bf16[2,256,768]{2,1,0:T(8,128)(2,1)}) custom-call(bf16[8,256,384]{2,1,0:T(8,128)(2,1)} %get-tuple-element.129.refs_0_.mixed, bf16[4,256,384]{2,1,0:T(8,128)(2,1)} %copy-done.25, ...), custom_call_target="tpu_custom_call" | custom-call | flops 1024 | bytes 21000000 | tf_op jit(solution)/shard_map/pallas_call | solution.py:642
  228.3 11.7 %collective-permute-done.30.rest_2_ = f32[2,392,128]{2,1,0:T(8,128)} collective-permute-done((f32[2,392,128]{2,1,0:T(8,128)S(1)}, f32[2,392,128]{2,1,0:T(8,128)}, u32[]{:S(2)}, u32[]{:S(2)}) %collective-permute-start.30) | collective-permute-done | bytes 401440 | tf_op jit(solution)/shard_map/ppermute | solution.py:38
  246.3 29.0 %shard_map.288 = (bf16[8,256,768]{2,1,0:T(8,128)(2,1)S(1)}, f32[2,16,640]{2,1,0:T(8,128)}, f32[2,8,640]{2,1,0:T(8,128)}, f32[8,640]{1,0:T(8,128)}) custom-call(s32[8]{0:T(128)S(1)} %stack.79.order, f32[8,256,640]{2,1,0:T(8,128)} %copy-done.2, f32[8,256,640]{2,1,0:T(8,128)} %get-tuple-element.135.conv, f32[8,256,640]{2,1,0:T(8,128)} %get-tuple-element.108.pre, ...), custom_call_target="tpu_custom_call" | custom-call | flops 1024 | bytes 98000000 | tf_op jit(solution)/shard_map/pallas_call | solution.py:799
  276.8 6.9 %collective-permute-done.31 = f32[2,8,640]{2,1,0:T(8,128)S(1)} collective-permute-done((f32[2,8,640]{2,1,0:T(8,128)}, f32[2,8,640]{2,1,0:T(8,128)S(1)}, u32[]{:S(2)}, u32[]{:S(2)}) %collective-permute-start.31) | collective-permute-done | bytes 40992 | tf_op jit(solution)/shard_map/ppermute | solution.py:38
  294.2 10.0 %shard_map.291 = (bf16[4,384,384]{2,1,0:T(8,128)(2,1)}, f32[4,128,384]{2,1,0:T(8,128)}, f32[4,128,384]{2,1,0:T(8,128)}, bf16[4,16,384]{2,1,0:T(8,128)(2,1)}) custom-call(s32[1]{0:T(128)} %bitcast.core, bf16[8,256,1536]{2,1,0:T(8,128)(2,1)} %get-tuple-element.116.tokens.refs_8_, bf16[8,256,768]{2,1,0:T(8,128)(2,1)S(1)} %slice_dynamic-update-slice_fusion.chan_low.refs_1_), custom_call_target="tpu_custom_call" | custom-call | flops 1024 | bytes 31500000 | tf_op jit(solution)/shard_map/pallas_call | solution.py:642
  317.3 14.5 %shard_map.293 = (f32[2,256,768]{2,1,0:T(8,128)S(1)}, f32[2,256,768]{2,1,0:T(8,128)S(1)}, bf16[2,256,768]{2,1,0:T(8,128)(2,1)S(1)}, bf16[2,256,768]{2,1,0:T(8,128)(2,1)S(1)}, f32[8,384]{1,0:T(8,128)}) custom-call(bf16[8,256,384]{2,1,0:T(8,128)(2,1)} %get-tuple-element.164.gate_low.refs_0_, ...), custom_call_target="tpu_custom_call" | custom-call | flops 1024 | bytes 38500000 | tf_op jit(solution)/shard_map/pallas_call | solution.py:642
  331.8 4.1 collective-permute-done.42.refs_2_
  339.4 5.6 %shard_map.290 = f32[2,256,1536]{2,1,0:T(8,128)} custom-call(s32[1]{0:T(128)} %bitcast.core, f32[256,1536]{1,0:T(8,128)} %pad_maximum_fusion.mine, f32[256,1536]{1,0:T(8,128)} %collective-permute-done.37.other, f32[2,256,1536]{2,1,0:T(8,128)} %base.2), custom_call_target="tpu_custom_call" | custom-call | flops 1024 | bytes 14000000 | tf_op jit(solution)/shard_map/pallas_call | solution.py:642
  345.0 10.4 %collective-permute-done.40.refs_1_ = bf16[528,384]{1,0:T(8,128)(2,1)S(1)} collective-permute-done((bf16[528,384]{1,0:T(8,128)(2,1)S(1)}, bf16[528,384]{1,0:T(8,128)(2,1)S(1)}, u32[]{:S(2)}, u32[]{:S(2)}) %collective-permute-start.40) | collective-permute-done | bytes 405536 | tf_op jit(solution)/shard_map/ppermute | solution.py:32
  377.5 4.3 %shard_map.296 = f32[2,256,1536]{2,1,0:T(8,128)} custom-call(s32[1]{0:T(128)} %bitcast.core, f32[256,1536]{1,0:T(8,128)S(1)} %fusion.2.mine, f32[256,1536]{1,0:T(8,128)S(1)} %collective-permute-done.49.other, f32[2,256,1536]{2,1,0:T(8,128)} %base.3), custom_call_target="tpu_custom_call" | custom-call | flops 1024 | bytes 14000000 | tf_op jit(solution)/shard_map/pallas_call | solution.py:642
  386.0 9.2 %collective-permute-done.51.refs_2_ = bf16[128,1424]{1,0:T(8,128)(2,1)S(1)} collective-permute-done((bf16[128,1424]{1,0:T(8,128)(2,1)S(1)}, bf16[128,1424]{1,0:T(8,128)(2,1)S(1)}, u32[]{:S(2)}, u32[]{:S(2)}) %collective-permute-start.51) | collective-permute-done | bytes 364576 | tf_op jit(solution)/shard_map/ppermute | solution.py:32
  (301 shorter events, 147.5 us)
Async XLA Ops:
  7.2 78.0 %all-gather.3.cloned.1.call-start = ((), (), s32[]{:S(2)}) async-start(), calls=%async_computation.1 | async-start | bytes 2949120 | tf_op jit(solution)/shard_map/all_gather | solution.py:887
  26.5 115.4 %all-gather.5.cloned.1.call-start = ((), (), s32[]{:S(2)}) async-start(), calls=%async_computation.2 | async-start | bytes 2949120 | tf_op jit(solution)/shard_map/all_gather | solution.py:890
  29.3 20.5 %collective-permute-start = (bf16[256,1536]{1,0:T(8,128)(2,1)S(1)}, bf16[256,1536]{1,0:T(8,128)(2,1)S(1)}, u32[]{:S(2)}, u32[]{:S(2)}) collective-permute-start(bf16[256,1536]{1,0:T(8,128)(2,1)S(1)} %dynamic-slice_bitcast_fusion.1), channel_id=1, source_target_pairs={{0,2},{2,0},{4,6},{6,4},{1,3},{3,1},{5,7},{7,5},{8,10},{10,8},{12,... | collective-permute-start | bytes 2359304 | tf_op jit(solution)/shard_map/ppermute | solution.py:32
  31.4 35.0 %collective-permute-start.1 = (bf16[256,1536]{1,0:T(8,128)(2,1)S(1)}, bf16[256,1536]{1,0:T(8,128)(2,1)S(1)}, u32[]{:S(2)}, u32[]{:S(2)}) collective-permute-start(bf16[256,1536]{1,0:T(8,128)(2,1)S(1)} %dynamic-slice_bitcast_fusion.1), channel_id=1, source_target_pairs={{0,4},{2,6},{4,0},{6,2},{1,5},{3,7},{5,1},{7,3},{8,12},{10,14},{12... | collective-permute-start | bytes 2359304 | tf_op jit(solution)/shard_map/ppermute | solution.py:32
  32.9 34.4 %collective-permute-start.2 = (bf16[256,1536]{1,0:T(8,128)(2,1)S(1)}, bf16[256,1536]{1,0:T(8,128)(2,1)}, u32[]{:S(2)}, u32[]{:S(2)}) collective-permute-start(bf16[256,1536]{1,0:T(8,128)(2,1)S(1)} %dynamic-slice_bitcast_fusion.1), channel_id=1, source_target_pairs={{0,6},{2,4},{4,2},{6,0},{1,7},{3,5},{5,3},{7,1},{8,14},{10,12},{12... | collective-permute-start | bytes 2359304 | tf_op jit(solution)/shard_map/ppermute | solution.py:32
  76.9 211.8 %reduce-scatter.2.cloned.1.call-start = ((), (), s32[]{:S(2)}) async-start(), calls=%async_computation.3 | async-start | bytes 2949120 | tf_op jit(solution)/shard_map/reduce_scatter | solution.py:1031
  81.7 59.5 %collective-permute-start.15 = (bf16[256,1536]{1,0:T(8,128)(2,1)S(1)}, bf16[256,1536]{1,0:T(8,128)(2,1)}, u32[]{:S(2)}, u32[]{:S(2)}) collective-permute-start(bf16[256,1536]{1,0:T(8,128)(2,1)S(1)} %dynamic-slice_bitcast_fusion), channel_id=1, source_target_pairs={{0,2},{2,0},{4,6},{6,4},{1,3},{3,1},{5,7},{7,5},{8,10},{10,8},{12,... | collective-permute-start | bytes 2359304 | tf_op jit(solution)/shard_map/ppermute | solution.py:32
  83.2 58.0 %collective-permute-start.16 = (bf16[256,1536]{1,0:T(8,128)(2,1)S(1)}, bf16[256,1536]{1,0:T(8,128)(2,1)}, u32[]{:S(2)}, u32[]{:S(2)}) collective-permute-start(bf16[256,1536]{1,0:T(8,128)(2,1)S(1)} %dynamic-slice_bitcast_fusion), channel_id=1, source_target_pairs={{0,4},{2,6},{4,0},{6,2},{1,5},{3,7},{5,1},{7,3},{8,12},{10,14},{12... | collective-permute-start | bytes 2359304 | tf_op jit(solution)/shard_map/ppermute | solution.py:32
  83.8 57.4 %collective-permute-start.17 = (bf16[256,1536]{1,0:T(8,128)(2,1)S(1)}, bf16[256,1536]{1,0:T(8,128)(2,1)}, u32[]{:S(2)}, u32[]{:S(2)}) collective-permute-start(bf16[256,1536]{1,0:T(8,128)(2,1)S(1)} %dynamic-slice_bitcast_fusion), channel_id=1, source_target_pairs={{0,6},{2,4},{4,2},{6,0},{1,7},{3,5},{5,3},{7,1},{8,14},{10,12},{12... | collective-permute-start | bytes 2359304 | tf_op jit(solution)/shard_map/ppermute | solution.py:32
  120.2 15.9 %collective-permute-start.10 = (f32[2,392,128]{2,1,0:T(8,128)}, f32[2,392,128]{2,1,0:T(8,128)}, u32[]{:S(2)}, u32[]{:S(2)}) collective-permute-start(f32[2,392,128]{2,1,0:T(8,128)} %get-tuple-element.115), channel_id=1, source_target_pairs={{0,8},{8,16},{16,24},{1,9},{9,17},{17,25},{2,10},{10,18},{18,26},{... | collective-permute-start | bytes 1204232 | tf_op jit(solution)/shard_map/ppermute | solution.py:38
  148.8 15.7 %collective-permute-start.21 = (f32[2,392,128]{2,1,0:T(8,128)}, f32[2,392,128]{2,1,0:T(8,128)}, u32[]{:S(2)}, u32[]{:S(2)}) collective-permute-start(f32[2,392,128]{2,1,0:T(8,128)} %collective-permute-done.14.rest_1_), channel_id=1, source_target_pairs={{0,8},{8,16},{16,24},{1,9},{9,17},{17,25},{2,10},{10,18},{18,26},{... | collective-permute-start | bytes 1204232 | tf_op jit(solution)/shard_map/ppermute | solution.py:38
  185.9 27.7 %collective-permute-start.27 = (bf16[1536,768]{1,0:T(8,128)(2,1)}, bf16[1536,768]{1,0:T(8,128)(2,1)}, u32[]{:S(2)}, u32[]{:S(2)}) collective-permute-start(bf16[1536,768]{1,0:T(8,128)(2,1)} %all-gather.5.cloned.1.call-done.table.refs_6_.refs_2_.refs_4_), channel_id=1, source_target_pairs={{0,1},{1,0},{2,3},{3,2},{4,5},{5,4},{6,7},{7,6},{8,9},{9,8},{10,11... | collective-permute-start | bytes 7077896 | tf_op jit(solution)/shard_map/ppermute | solution.py:32
  196.8 15.4 %collective-permute-start.26 = (f32[2,392,128]{2,1,0:T(8,128)}, f32[2,392,128]{2,1,0:T(8,128)S(1)}, u32[]{:S(2)}, u32[]{:S(2)}) collective-permute-start(f32[2,392,128]{2,1,0:T(8,128)} %get-tuple-element.130), channel_id=1, source_target_pairs={{8,0},{16,8},{24,16},{9,1},{17,9},{25,17},{10,2},{18,10},{26,18},{... | collective-permute-start | bytes 1204232 | tf_op jit(solution)/shard_map/ppermute | solution.py:38
  240.1 48.6 %collective-permute-start.32 = (bf16[2,256,768]{2,1,0:T(8,128)(2,1)}, bf16[2,256,768]{2,1,0:T(8,128)(2,1)}, u32[]{:S(2)}, u32[]{:S(2)}) collective-permute-start(bf16[2,256,768]{2,1,0:T(8,128)(2,1)} %get-tuple-element.137), channel_id=1, source_target_pairs={{0,2},{2,0},{4,6},{6,4},{1,3},{3,1},{5,7},{7,5},{8,10},{10,8},{12,... | collective-permute-start | bytes 2359304 | tf_op jit(solution)/shard_map/ppermute | solution.py:32
  241.8 46.9 %collective-permute-start.33 = (bf16[2,256,768]{2,1,0:T(8,128)(2,1)}, bf16[2,256,768]{2,1,0:T(8,128)(2,1)}, u32[]{:S(2)}, u32[]{:S(2)}) collective-permute-start(bf16[2,256,768]{2,1,0:T(8,128)(2,1)} %get-tuple-element.138), channel_id=1, source_target_pairs={{0,4},{2,6},{4,0},{6,2},{1,5},{3,7},{5,1},{7,3},{8,12},{10,14},{12... | collective-permute-start | bytes 2359304 | tf_op jit(solution)/shard_map/ppermute | solution.py:32
  244.3 47.0 %collective-permute-start.34 = (bf16[4,256,384]{2,1,0:T(8,128)(2,1)}, bf16[4,256,384]{2,1,0:T(8,128)(2,1)}, u32[]{:S(2)}, u32[]{:S(2)}) collective-permute-start(bf16[4,256,384]{2,1,0:T(8,128)(2,1)} %slice.135), channel_id=1, source_target_pairs={{0,1},{1,0},{2,3},{3,2},{4,5},{5,4},{6,7},{7,6},{8,9},{9,8},{10,11... | collective-permute-start | bytes 2359304 | tf_op jit(solution)/shard_map/ppermute | solution.py:32
  309.8 29.6 %collective-permute-start.37 = (f32[256,1536]{1,0:T(8,128)}, f32[256,1536]{1,0:T(8,128)}, u32[]{:S(2)}, u32[]{:S(2)}) collective-permute-start(f32[256,1536]{1,0:T(8,128)} %pad_maximum_fusion.mine), channel_id=1, source_target_pairs={{0,1},{1,0},{2,3},{3,2},{4,5},{5,4},{6,7},{7,6},{8,9},{9,8},{10,11... | collective-permute-start | bytes 4718600 | tf_op jit(solution)/shard_map/ppermute | solution.py:32
  313.9 17.9 %collective-permute-start.41 = (bf16[528,384]{1,0:T(8,128)(2,1)}, bf16[528,384]{1,0:T(8,128)(2,1)S(1)}, u32[]{:S(2)}, u32[]{:S(2)}) collective-permute-start(bf16[528,384]{1,0:T(8,128)(2,1)} %get-tuple-element.173), channel_id=1, source_target_pairs={{0,8},{8,0},{16,24},{24,16},{1,9},{9,1},{17,25},{25,17},{2,10},{10... | collective-permute-start | bytes 1216520 | tf_op jit(solution)/shard_map/ppermute | solution.py:32
  314.4 21.6 %collective-permute-start.42 = (bf16[528,384]{1,0:T(8,128)(2,1)}, bf16[528,384]{1,0:T(8,128)(2,1)S(1)}, u32[]{:S(2)}, u32[]{:S(2)}) collective-permute-start(bf16[528,384]{1,0:T(8,128)(2,1)} %get-tuple-element.174), channel_id=1, source_target_pairs={{0,24},{8,16},{16,8},{24,0},{1,25},{9,17},{17,9},{25,1},{2,26},{10... | collective-permute-start | bytes 1216520 | tf_op jit(solution)/shard_map/ppermute | solution.py:32
  336.0 19.5 %collective-permute-start.43 = (bf16[2,256,768]{2,1,0:T(8,128)(2,1)S(1)}, bf16[2,256,768]{2,1,0:T(8,128)(2,1)S(1)}, u32[]{:S(2)}, u32[]{:S(2)}) collective-permute-start(bf16[2,256,768]{2,1,0:T(8,128)(2,1)S(1)} %get-tuple-element.175), channel_id=1, source_target_pairs={{0,2},{2,0},{4,6},{6,4},{1,3},{3,1},{5,7},{7,5},{8,10},{10,8},{12,... | collective-permute-start | bytes 2359304 | tf_op jit(solution)/shard_map/ppermute | solution.py:32
  336.5 18.9 %collective-permute-start.44 = (bf16[2,256,768]{2,1,0:T(8,128)(2,1)S(1)}, bf16[2,256,768]{2,1,0:T(8,128)(2,1)S(1)}, u32[]{:S(2)}, u32[]{:S(2)}) collective-permute-start(bf16[2,256,768]{2,1,0:T(8,128)(2,1)S(1)} %get-tuple-element.176), channel_id=1, source_target_pairs={{0,4},{2,6},{4,0},{6,2},{1,5},{3,7},{5,1},{7,3},{8,12},{10,14},{12... | collective-permute-start | bytes 2359304 | tf_op jit(solution)/shard_map/ppermute | solution.py:32
  337.1 18.4 %collective-permute-start.40 = (bf16[528,384]{1,0:T(8,128)(2,1)S(1)}, bf16[528,384]{1,0:T(8,128)(2,1)S(1)}, u32[]{:S(2)}, u32[]{:S(2)}) collective-permute-start(bf16[528,384]{1,0:T(8,128)(2,1)S(1)} %copy-done.45), channel_id=1, source_target_pairs={{0,16},{8,24},{16,0},{24,8},{1,17},{9,25},{17,1},{25,9},{2,18},{10... | collective-permute-start | bytes 1216520 | tf_op jit(solution)/shard_map/ppermute | solution.py:32
  338.4 22.9 %collective-permute-start.45 = (f32[24,640]{1,0:T(8,128)S(1)}, f32[24,640]{1,0:T(8,128)S(1)}, u32[]{:S(2)}, u32[]{:S(2)}) collective-permute-start(f32[24,640]{1,0:T(8,128)S(1)} %select_maximum_fusion), channel_id=1, source_target_pairs={{0,8},{8,0},{16,24},{24,16},{1,9},{9,1},{17,25},{25,17},{2,10},{10... | collective-permute-start | bytes 184328 | tf_op jit(solution)/shard_map/ppermute | solution.py:32
  376.2 19.1 %collective-permute-start.51 = (bf16[128,1424]{1,0:T(8,128)(2,1)S(1)}, bf16[128,1424]{1,0:T(8,128)(2,1)S(1)}, u32[]{:S(2)}, u32[]{:S(2)}) collective-permute-start(bf16[128,1424]{1,0:T(8,128)(2,1)S(1)} %copy-done.47), channel_id=1, source_target_pairs={{0,4},{2,6},{4,0},{6,2},{1,5},{3,7},{5,1},{7,3},{8,12},{10,14},{12... | collective-permute-start | bytes 1093640 | tf_op jit(solution)/shard_map/ppermute | solution.py:32
  (85 other events, 850.8 us)
Sparse Core Ops, SparseCore 0:
  26.6 52.1 all-gather.2
  80.9 49.4 all-gather.4
  240.1 48.5 reduce-scatter.1
